TPU v7x, 128 devices: a whole 4x4x4 slice. The times are simulated.
128 devices in a mesh: series: 4 (over x), tm: 32 (over z, y, core).
Axes of the slice: x: 4, y: 4, z: 4, core: 2. Of those that a mesh axis runs over, the one named last changes fastest.
Arguments:
- raw_values: float32 [4, 4096], P('series', 'tm'), may hold values from -6 to 6
- hours: int32 [4, 4096], P('series', 'tm'), may hold values from 0 to 23
- doc_lengths: int32 [4, 7], P('series'), may hold values from 16 to 4000, as said below
- doc_scale: float32 [4, 7], P('series'), may hold values from 0.5 to 2
- dataset_ids: int32 [4, 7, 1], P('series'), may hold values from 0 to 7
- lag_offsets: int32 [84], replicated, may hold values from 1 to 384, as said below
- w_lag: bfloat16 [87, 144], replicated, may hold values from -0.625 to 0.625
- w_qkv: bfloat16 [2, 144, 432], replicated, may hold values from -0.5 to 0.5
- w_out: bfloat16 [2, 144, 144], replicated, may hold values from -1.5 to 1.5
- w_gate_up: bfloat16 [2, 144, 768], replicated, may hold values from -0.5 to 0.5
- w_down: bfloat16 [2, 384, 144], replicated, may hold values from -0.3125 to 0.3125
- gains: float32 [2, 2, 144], replicated, may hold values from 0.5 to 1.5
- cotangent: float32 [4, 4096, 144], P('series', 'tm'), may hold values from -6 to 6
Outputs:
- activations: float32 [4, 4096, 144], P('series', 'tm')
- raw_grad: float32 [4, 4096], P('series', 'tm')
- scale_mean: float32 [8], replicated
- w_lag_grad: float32 [87, 144], replicated
- w_qkv_grad: float32 [2, 144, 432], replicated
- w_out_grad: float32 [2, 144, 144], replicated
- w_gate_up_grad: float32 [2, 144, 768], replicated
- w_down_grad: float32 [2, 384, 144], replicated
- gains_grad: float32 [2, 2, 144], replicated
Inputs may be any that keep to these rules, and one draw needn't show every extreme that they name: `doc_lengths`: each row holds 3 short series, then one long series, then 3 short series; short ones have 32 // 2 to 32 steps; the row sums to 4096. `lag_offsets`: distinct and rising, the last equal to 384.
All inputs are finite; a program needn't handle non-finite values.
Results may differ from a plain program's by a relative error of at most 0.025.
Values may be sent and summed in bfloat16 or wider, within the bound.
No kernel may reach another device: no remote copies, remote signals or barrier semaphores. Data moves between devices by JAX's collectives and lax.ppermute only.
A program may use at most 192 MiB of HBM per device.

v0:
```python
import math

import jax
import jax.numpy as jnp
import numpy as np
from jax import lax
from jax.experimental import pallas as pl
from jax.experimental.pallas import tpu as pltpu
from jax.sharding import PartitionSpec as P


D = 144
HEADS = 9
HEAD_DIM = 16
FF = 384
LAGS = 84
LAYERS = 2
DATASETS = 8
DOCS = 7
LEN = 4096
MAXLAG = 384
FEATS = 87
EPSILON = 1e-06
MASKED = -1e30
AUG = 192
STAT = AUG - D
LROW = D
DROW = D + 27
BLOCK = 512
BLOCKS = LEN // BLOCK
TILE = 128
TILES = LEN // TILE
STEPS = BLOCKS + 1
UNROLL = 3
HALF = 64
ROWS = HEADS * HALF
LAGCOLS = 400
EARLY = 103
LATE = 24
WIDE = AUG + HALF
SAFE = 40.0
VMEM = 28 * 2**20

bf16 = jnp.bfloat16
f32 = jnp.float32
HIGH = lax.Precision.HIGHEST


def nn(a, b, precision=None):
    return lax.dot_general(a, b, (((1,), (0,)), ((), ())), precision=precision, preferred_element_type=f32)


def nt(a, b, precision=None):
    return lax.dot_general(a, b, (((1,), (1,)), ((), ())), precision=precision, preferred_element_type=f32)


def tn(a, b, precision=None):
    return lax.dot_general(a, b, (((0,), (0,)), ((), ())), precision=precision, preferred_element_type=f32)


def iota(shape, dim):
    return lax.broadcasted_iota(jnp.int32, shape, dim)


def eye(rows, cols, dtype):
    return (iota((rows, cols), 0) == iota((rows, cols), 1)).astype(dtype)


def column(row, size):
    keep = iota((size, size), 0) == iota((size, size), 1)
    return jnp.sum(jnp.where(keep, row, 0.0), axis=1, keepdims=True)


def pair_of(chip):
    return jnp.where(chip < 8, 2 * chip, TILES - 1 - 2 * chip)


def geometry():
    index = lax.axis_index("tm")
    chip, core = index // 2, index % 2
    tile = pair_of(chip)
    low = jnp.where(core == 0, tile, TILES - 1 - tile)
    return chip, core, low, TILES - 1 - low


def doc_start(places, len_ref):
    start = jnp.zeros_like(places)
    end = jnp.int32(0)
    for d in range(DOCS):
        end = end + len_ref[d]
        start = jnp.where(places >= end, end, start)
    return start


def doc_scale_at(places, len_ref, scale_ref):
    own = jnp.full(places.shape, scale_ref[0], f32)
    end = jnp.int32(0)
    for d in range(1, DOCS):
        end = end + len_ref[d - 1]
        own = jnp.where(places >= end, scale_ref[d], own)
    return own


def own_places(low, high):
    lane = iota((1, TILE), 1)
    return jnp.where(lane < HALF, low, high) * TILE + lane


def half_places(u, tile):
    return iota((HALF, 1), 0) + (tile * TILE + u * HALF)


def rotate(x, cosine, sine):
    cols = x.shape[1]
    parts = x.reshape(HEADS, 2, 8, cols)
    one, two = parts[:, 0], parts[:, 1]
    turned = jnp.stack([one * cosine - two * sine, two * cosine + one * sine], axis=1)
    return turned.reshape(D, cols)


def norm_factor(x):
    return lax.rsqrt(jnp.mean(x * x, axis=0, keepdims=True) + EPSILON)


def norm_back(x, gain, d_normal):
    r = norm_factor(x)
    scaled = d_normal * gain
    inner = jnp.mean(x * scaled, axis=0, keepdims=True)
    d_x = r * scaled - (r * r * r * inner) * x
    return d_x, jnp.sum(d_normal * x * r, axis=1, keepdims=True)


def head_columns(h, *firsts):
    col = iota((1, AUG), 1)
    keep = (col >= h * HEAD_DIM) & (col < (h + 1) * HEAD_DIM)
    for first in firsts:
        keep = keep | (col == first + h)
    return keep


def spread(ref, rows, *firsts):
    zero = jnp.zeros((HALF, AUG), f32)
    for h in range(HEADS):
        keep = head_columns(h, *firsts)
        for u in range(2):
            part = rows[u * HALF : (u + 1) * HALF]
            ref[u, h * HALF : (h + 1) * HALF, 0:AUG] = jnp.where(keep, part, zero).astype(bf16)
    if ref.shape[2] == WIDE:
        unit = eye(HALF, HALF, bf16)
        for h in range(HEADS):
            for u in range(2):
                ref[u, h * HALF : (h + 1) * HALF, AUG:WIDE] = unit


def own_heads(x):
    col = iota((1, D), 1) // HEAD_DIM
    total = jnp.zeros((HALF, D), f32)
    for h in range(HEADS):
        total = jnp.where(col == h, x[h * HALF : (h + 1) * HALF, :D], total)
    return total


def three_parts(x):
    hi = x.astype(bf16)
    rest = x - hi.astype(f32)
    mid = rest.astype(bf16)
    return hi, mid, (rest - mid.astype(f32)).astype(bf16)


class Tiles:
    def __init__(self, ref):
        self.ref, self.count = ref, 0

    def tile(self, value):
        self.ref[self.count] = value.astype(bf16)
        self.count += 1

    def __call__(self, grads):
        for c in range(grads.shape[1] // TILE):
            for r in range(grads.shape[0] // 16):
                self.tile(grads[16 * r : 16 * (r + 1), c * TILE : (c + 1) * TILE].astype(f32))


class Pairs(Tiles):
    def __init__(self, core, keep_ref, send_ref, rest_ref=None):
        self.core, self.refs, self.rest, self.count, self.even = core, (keep_ref, send_ref), rest_ref, 0, None

    def tile(self, value):
        if self.count == self.refs[0].shape[0]:
            self.rest[0] = value.astype(bf16)
        elif self.even is None:
            self.even = value
        else:
            self.refs[0][self.count] = jnp.where(self.core == 0, self.even, value).astype(bf16)
            self.refs[1][self.count] = jnp.where(self.core == 0, value, self.even).astype(bf16)
            self.even = None
            self.count += 1


def turned(w):
    return tn(w, eye(D, D, bf16)).astype(bf16)


def key_value_block(normal, w_qkv, rope_ref, k, kaug_ref, vaug_ref):
    mixed = nn(w_qkv[D:], normal)
    at = slice(k * BLOCK, (k + 1) * BLOCK)
    keys = rotate(mixed[:D], rope_ref[0:8, at], rope_ref[8:16, at])
    ones = jnp.ones((STAT, BLOCK), bf16)
    kaug_ref[k, 0:D, :] = keys.astype(bf16)
    vaug_ref[k, 0:D, :] = mixed[D:].astype(bf16)
    kaug_ref[k, D:AUG, :] = ones
    vaug_ref[k, D:AUG, :] = ones
    return head_sizes(keys)


def query_of(normal, w_qkv, cosine, sine):
    turned = rotate(nn(w_qkv[:D], normal), cosine, sine)
    return (turned.astype(bf16).astype(f32) * HEAD_DIM**-0.5).astype(bf16)


def own_rope(rope_ref, low, high):
    def at(tile):
        return rope_ref[:, pl.ds(pl.multiple_of(tile * TILE, TILE), TILE)]

    both = jnp.where(iota((1, TILE), 1) < HALF, at(low), at(high))
    return both[0:8], both[8:16]


def own_tile(ref, low, high):
    lane = iota((1, TILE), 1)

    def at(tile):
        return ref[tile // 4, 0:D, pl.ds(pl.multiple_of((tile % 4) * TILE, TILE), TILE)].astype(f32)

    return jnp.where(lane < HALF, at(low), at(high)).astype(bf16)


def query_bias(u, tile, block, len_ref):
    places = half_places(u, tile)
    start = doc_start(places, len_ref)
    keys = iota((1, BLOCK), 1) + block * BLOCK
    return jnp.where((keys <= places) & (keys >= start), 0.0, MASKED).astype(bf16)


def key_bias(u, tile, block, len_ref):
    keys = half_places(u, tile)
    places = iota((1, BLOCK), 1) + block * BLOCK
    start = doc_start(places, len_ref)
    return jnp.where((keys <= places) & (keys >= start), 0.0, MASKED).astype(bf16)


def scores_of(rows, columns, bias):
    return nn(rows, jnp.concatenate([columns, bias], axis=0))


def run_steps(step):
    def several(i, carry):
        for j in range(UNROLL):
            step(i * UNROLL + j)
        return carry

    lax.fori_loop(0, STEPS // UNROLL, several, 0)


def query_step(s, low, high):
    first = low // 4 + 1
    late = s >= first
    return late.astype(jnp.int32), jnp.where(late, high, low), s - jnp.where(late, first, 0)


def key_step(s, low, high):
    first = BLOCKS - low // 4
    late = s >= first
    tile = jnp.where(late, high, low)
    return late.astype(jnp.int32), tile, tile // 4 + s - jnp.where(late, first, 0)


def head_sizes(x):
    return jnp.max(jnp.sum((x * x).reshape(HEADS, HEAD_DIM, x.shape[1]), axis=1), axis=1, keepdims=True)


def attend(query, k_size, kaug_ref, vaug_ref, len_ref, low, high, qbd, top_ref, acc_ref, q_rows_ref):
    q_rows = nt(eye(TILE, TILE, bf16), query)
    q_rows_ref[...] = q_rows.astype(bf16)
    spread(qbd, jnp.concatenate([q_rows, jnp.zeros((TILE, STAT), f32)], axis=1))
    q_size = head_sizes(query.astype(f32))
    acc_ref[...] = jnp.zeros(acc_ref.shape, f32)
    safe = jnp.max(q_size * k_size) <= SAFE * SAFE

    @pl.when(safe)
    def _():
        top_ref[...] = jnp.zeros(top_ref.shape, f32)

        def step(s):
            u, tile, block = query_step(s, low, high)
            scores = scores_of(qbd[u], kaug_ref[block], query_bias(u, tile, block, len_ref))
            acc_ref[u] = acc_ref[u] + nt(jnp.exp(scores).astype(bf16), vaug_ref[block])

        run_steps(step)

    @pl.when(jnp.logical_not(safe))
    def _():
        top_ref[...] = jnp.full(top_ref.shape, MASKED, f32)

        def step(s, carry):
            u, tile, block = query_step(s, low, high)
            scores = scores_of(qbd[u], kaug_ref[block], query_bias(u, tile, block, len_ref))
            old = top_ref[u]
            new = jnp.maximum(old, jnp.max(scores, axis=1, keepdims=True))
            probs = jnp.exp(scores - new)
            acc_ref[u] = acc_ref[u] * jnp.exp(old - new) + nt(probs.astype(bf16), vaug_ref[block])
            top_ref[u] = new
            return carry

        lax.fori_loop(0, STEPS, step, 0)

    attended, stats = [], []
    lane = iota((1, STAT), 1)
    for u in range(2):
        acc = acc_ref[u]
        total = acc[:, D : D + 1]
        attended.append(own_heads(acc[:, :D] / total))
        parts = three_parts(-(top_ref[u] + jnp.log(total)))
        stat = jnp.zeros((HALF, STAT), f32)
        for j in range(3):
            part = parts[j].astype(f32)
            for h in range(HEADS):
                stat = jnp.where(lane == 9 * j + h, part[h * HALF : (h + 1) * HALF], stat)
        stats.append(stat)
    att_rows = jnp.concatenate(attended, axis=0).astype(bf16)
    stat_rows = jnp.concatenate(stats, axis=0).astype(bf16)
    return nt(eye(D, D, bf16), att_rows).astype(bf16), nt(eye(STAT, STAT, bf16), stat_rows).astype(bf16)


def feed_forward(resid, attended, w_out, w_gate_up, w_down, gain):
    mid = resid + nn(w_out, attended)
    normal = (mid * norm_factor(mid) * gain).astype(bf16)
    gate_up = nn(w_gate_up, normal)
    gate = gate_up[:FF]
    hidden = (gate * jax.nn.sigmoid(gate) * gate_up[FF:]).astype(bf16)
    return mid, normal, gate_up, hidden, mid + nn(w_down, hidden)


def feed_back(grad, attended, mid, gate_up, w_out, w_gate_up, w_down, gain, stat, low_refs, traffic):
    d_out_ref, d_gate_up_ref, d_branch_ref, hidden_ref, normal_ref = low_refs
    d_out = grad.astype(bf16)
    d_hidden = tn(w_down, d_out)
    gate, up = gate_up[:FF], gate_up[FF:]
    sig = jax.nn.sigmoid(gate)
    d_gate = d_hidden * up * (sig * (1.0 + gate * (1.0 - sig)))
    d_up = d_hidden * (gate * sig)
    hidden_ref[...] = (gate * sig * up).astype(bf16)
    normal_ref[...] = (mid * norm_factor(mid) * gain).astype(bf16)
    d_gate_up = jnp.concatenate([d_gate, d_up], axis=0).astype(bf16)
    d_mid, d_gain = norm_back(mid, gain, nn(w_gate_up, d_gate_up))
    grad = grad + d_mid
    d_branch = grad.astype(bf16)
    d_att = nn(w_out, d_branch).astype(bf16)
    d_out_ref[...], d_gate_up_ref[...], d_branch_ref[...] = d_out, d_gate_up, d_branch
    traffic.send(*low_refs)
    product = d_att.astype(f32) * attended.astype(f32)
    delta = -jnp.sum(product.reshape(HEADS, HEAD_DIM, TILE), axis=1)
    delta = jnp.concatenate([delta, jnp.zeros((16 - HEADS, TILE), f32)], axis=0)
    hi, lo, _ = three_parts(delta)
    row, col = iota((STAT, 16), 0), iota((STAT, 16), 1)
    place = [((row == 27 + 9 * j + col) & (col < HEADS)).astype(bf16) for j in range(2)]
    stat = stat.astype(f32) + nn(place[0], hi) + nn(place[1], lo)
    return grad, jnp.concatenate([d_att, stat.astype(bf16)], axis=0), d_gain


def feed_grads(put, hidden, d_out, normal, d_gate_up, attended, d_branch):
    put(nt(d_out, hidden))
    put(nt(normal, d_gate_up))
    put(nt(attended, d_branch[:TILE]))
    rows = [jnp.zeros((48, TILE), bf16), d_branch[TILE:], jnp.zeros((TILE - 64, TILE), bf16)]
    return nt(attended, jnp.concatenate(rows, axis=0))


def gain_column(gains_ref, which):
    return column(gains_ref[which // 2, which % 2 : which % 2 + 1, :], D)


def first_kernel(
    traffic, values_ref, len_ref, scale_ref, lag_ref, w_lag_ref, w_qkv_ref, w_out_ref, w_gate_up_ref, w_down_ref, gains_ref, rope_ref,
    copies_ref, next_ref, next_resid_ref, kaug_ref, vaug_ref, normal_all, lagged_ref, feats_ref, w_dense_ref, resid_ref, normal_a_ref,
    q_ref, att_ref, stat_ref, mid_ref, gate_up_ref,
    series, toeplitz, extra, qbd, top_ref, acc_ref,
):
    chip, core, low, high = geometry()
    traffic.ready(2)
    places = iota((TILES, TILE), 0) * TILE + iota((TILES, TILE), 1)
    own = doc_scale_at(places, len_ref, scale_ref)
    values = values_ref[:, 0, :] / own
    angle = values_ref[:, 1, :] * (2.0 * math.pi / 24.0)
    sine, cosine, level = jnp.sin(angle), jnp.cos(angle), jnp.log(own)
    series[0:8, :] = jnp.zeros((8, TILE), f32)
    series[8 : 8 + TILES, :] = values.astype(bf16).astype(f32)
    extra[...] = jnp.zeros(extra.shape, f32)
    for r in range(TILES):
        at = slice(r * TILE, (r + 1) * TILE)
        extra[0:1, at] = sine[r : r + 1]
        extra[1:2, at] = cosine[r : r + 1]
        extra[2:3, at] = level[r : r + 1]
    toeplitz[:, 0:MAXLAG] = jnp.zeros((TILE, MAXLAG), bf16)

    def shift(m, carry):
        window = jnp.concatenate([series[pl.ds(m + 7, 1), :], series[pl.ds(m + 8, 1), :]], axis=1)
        rolled = pltpu.roll(jnp.broadcast_to(window, (TILE, 2 * TILE)), 1, 1, stride=1, stride_axis=0)
        toeplitz[:, pl.ds(pl.multiple_of((m + 3) * TILE, TILE), TILE)] = rolled[:, TILE:].astype(bf16)
        return carry

    lax.fori_loop(0, TILES, shift, 0, unroll=4)

    traffic.ready()

    rows = iota((FEATS, 1), 0)
    diagonal = iota((FEATS, LAGS), 0) == iota((FEATS, LAGS), 1)
    offsets = jnp.sum(jnp.where(diagonal, lag_ref[...].astype(f32), 0.0), axis=1, keepdims=True)
    offsets = jnp.where(rows < LAGS, offsets - 1.0, (rows - LAGS + MAXLAG).astype(f32))
    chosen = (iota((FEATS, LAGCOLS), 1).astype(f32) == offsets).astype(bf16)
    w_dense = nn(w_lag_ref[...], chosen).astype(bf16)
    w_dense_ref[...] = w_dense

    gain_a, gain_b = gain_column(gains_ref, 0), gain_column(gains_ref, 1)
    w_qkv = turned(w_qkv_ref[0])
    lag_rows = iota((TILE, 1), 0) + 1
    k_size = jnp.zeros((HEADS, 1), f32)
    for k in range(BLOCKS):
        place = iota((1, BLOCK), 1) + k * BLOCK
        start = doc_start(place, len_ref)
        parts = []
        for b in range(3):
            at = MAXLAG + k * BLOCK - b * TILE
            lagged = toeplitz[:, at : at + BLOCK]
            if k in (0, BLOCKS - 1):
                valid = place - (lag_rows + b * TILE) >= start
                lagged = jnp.where(valid, lagged.astype(f32), 0.0).astype(bf16)
            parts.append(lagged)
        parts.append(extra[:, k * BLOCK : (k + 1) * BLOCK].astype(bf16))
        resid = nn(w_dense, jnp.concatenate(parts, axis=0))
        normal = (resid * norm_factor(resid) * gain_a).astype(bf16)
        normal_all[k] = normal
        k_size = jnp.maximum(k_size, key_value_block(normal, w_qkv, rope_ref, k, kaug_ref, vaug_ref))

    traffic.send(kaug_ref, vaug_ref, normal_all, w_dense_ref)

    place = own_places(low, high)
    start = doc_start(place, len_ref)
    lane = iota((1, TILE), 1)

    def tile_of(ref, tile):
        return ref[:, pl.ds(pl.multiple_of(tile * TILE, TILE), TILE)].astype(f32)

    for b in range(3):
        lagged = jnp.where(lane < HALF, tile_of(toeplitz, low + 3 - b), tile_of(toeplitz, high + 3 - b))
        valid = place - (lag_rows + b * TILE) >= start
        lagged_ref[b * TILE : (b + 1) * TILE, :] = jnp.where(valid, lagged, 0.0).astype(bf16)
    lagged_ref[MAXLAG:, :] = jnp.where(lane < HALF, tile_of(extra, low), tile_of(extra, high)).astype(bf16)
    lagged = lagged_ref[...]
    feats_ref[0:FEATS, :] = nn(chosen, lagged)
    feats_ref[FEATS:, :] = jnp.zeros((96 - FEATS, TILE), f32)
    resid = nn(w_dense, lagged)
    resid_ref[...] = resid
    normal = (resid * norm_factor(resid) * gain_a).astype(bf16)
    normal_a_ref[...] = normal
    traffic.send(lagged_ref, feats_ref, resid_ref, normal_a_ref)
    query = query_of(normal, w_qkv, *own_rope(rope_ref, low, high))
    attended, stat_ref[...] = attend(query, k_size, kaug_ref, vaug_ref, len_ref, low, high, qbd, top_ref, acc_ref, q_ref)
    att_ref[...] = attended
    traffic.send(q_ref, att_ref, stat_ref)
    mid, _, gate_up, _, resid = feed_forward(
        resid, attended, turned(w_out_ref[0]), turned(w_gate_up_ref[0]), w_down_ref[0], gain_b
    )
    mid_ref[...], gate_up_ref[...] = mid, gate_up
    traffic.send(mid_ref, gate_up_ref)
    next_resid_ref[...] = resid
    normal = (resid * norm_factor(resid) * gain_column(gains_ref, 2)).astype(bf16)
    next_ref[...] = normal
    copies_ref[...] = jnp.broadcast_to(normal[None], copies_ref.shape)


def natural_tiles(own_ref, other_ref, put):
    _, core, _, _ = geometry()
    mine = (iota((1, TILE), 1) < HALF) == (core == 0)
    for chip in range(TILES // 2):
        tile = 2 * chip if chip < 8 else TILES - 1 - 2 * chip
        own, other = own_ref[chip].astype(f32), other_ref[chip].astype(f32)
        for t, value in ((tile, jnp.where(mine, own, other)), (TILES - 1 - tile, jnp.where(mine, other, own))):
            put(t // 4, slice(t % 4 * TILE, (t % 4 + 1) * TILE), value.astype(bf16))


def second_kernel(
    traffic, own_ref, other_ref, len_ref, cot_own_ref, cot_other_ref, normal_ref, resid_in_ref, turned_qkv_ref, turned_out_ref,
    turned_gate_up_ref, w_out_ref, w_gate_up_ref, w_down_ref, gains_ref, rope_ref,
    copies_ref, act_ref, kaug_ref, vaug_ref, normal_all, q_ref, grad_ref, payload_ref, att_ref, d_gain_ref,
    d_out_ref, d_gate_up_ref, d_branch_ref, hidden_ref, normal_b_ref,
    qbd, top_ref, acc_ref,
):
    chip, core, low, high = geometry()

    def put(block, columns, value):
        normal_all[block, :, columns] = value

    natural_tiles(own_ref, other_ref, put)
    traffic.send(normal_all)
    traffic.ready()
    w_qkv = turned_qkv_ref[1]
    k_size = jnp.zeros((HEADS, 1), f32)
    for k in range(BLOCKS):
        k_size = jnp.maximum(k_size, key_value_block(normal_all[k], w_qkv, rope_ref, k, kaug_ref, vaug_ref))
    traffic.send(kaug_ref, vaug_ref)
    query = query_of(normal_ref[...], w_qkv, *own_rope(rope_ref, low, high))
    attended, stat = attend(query, k_size, kaug_ref, vaug_ref, len_ref, low, high, qbd, top_ref, acc_ref, q_ref)
    gain = gain_column(gains_ref, 3)
    w_out, w_gate_up, w_down = w_out_ref[1], w_gate_up_ref[1], w_down_ref[1]
    mid, _, gate_up, _, out = feed_forward(
        resid_in_ref[...], attended, turned_out_ref[1], turned_gate_up_ref[1], w_down, gain
    )
    act_ref[...] = out
    att_ref[...] = attended
    traffic.send(act_ref, att_ref, q_ref)
    grad = tile_halves(cot_own_ref[...].astype(f32), cot_other_ref[...].astype(f32))
    low_refs = (d_out_ref, d_gate_up_ref, d_branch_ref, hidden_ref, normal_b_ref)
    grad, payload, d_gain_ref[...] = feed_back(grad, attended, mid, gate_up, w_out, w_gate_up, w_down, gain, stat, low_refs, traffic)
    grad_ref[...] = grad
    payload_ref[...] = payload
    copies_ref[...] = jnp.broadcast_to(payload[None], copies_ref.shape)


def query_back(
    traffic, count, layer, payload_ref, q_ref, len_ref, rope_ref, kaug_ref, vaug_ref, normal_all, w_qkv_ref, dq_ref, qall_ref, kbd, vbd,
    qbd, dbd, acc_ref,
):
    chip, core, low, high = geometry()
    traffic.ready(count)
    unit = eye(TILE, TILE, bf16)
    rows = nt(unit, payload_ref[...])
    spread(qbd, jnp.concatenate([q_ref[...].astype(f32), rows[:, D:]], axis=1), LROW, LROW + 9, LROW + 18)
    spread(dbd, rows, DROW, DROW + 9)
    ones = jnp.ones((TILE, STAT), f32)
    spread(kbd, jnp.concatenate([nt(unit, own_tile(kaug_ref, low, high)), ones], axis=1), LROW, LROW + 9, LROW + 18)
    spread(vbd, jnp.concatenate([nt(unit, own_tile(vaug_ref, low, high)), ones], axis=1), DROW, DROW + 9)
    w_qkv = w_qkv_ref[layer]
    for k in range(BLOCKS):
        at = slice(k * BLOCK, (k + 1) * BLOCK)
        qall_ref[k] = query_of(normal_all[k], w_qkv, rope_ref[0:8, at], rope_ref[8:16, at])
    traffic.send(kbd, vbd, qall_ref)
    acc_ref[...] = jnp.zeros(acc_ref.shape, f32)

    def step(s):
        u, tile, block = query_step(s, low, high)
        scores = scores_of(qbd[u], kaug_ref[block], query_bias(u, tile, block, len_ref))
        d_scores = jnp.exp(scores) * nn(dbd[u], vaug_ref[block])
        acc_ref[u] = acc_ref[u] + nt(d_scores.astype(bf16), kaug_ref[block])

    run_steps(step)
    d_query = jnp.concatenate([own_heads(acc_ref[0]), own_heads(acc_ref[1])], axis=0) * HEAD_DIM**-0.5
    cosine, sine = own_rope(rope_ref, low, high)
    dq_ref[...] = rotate(nt(eye(D, D, f32), d_query, HIGH), cosine, -sine)


def key_back(traffic, own_ref, other_ref, len_ref, qall_ref, kbd, vbd, dq_ref, grad_ref, resid_ref, layer, w_qkv_ref, gains_ref, rope_ref, daug, dk_ref, dv_ref):
    chip, core, low, high = geometry()

    def put(block, columns, value):
        daug[block, :, columns] = value

    natural_tiles(own_ref, other_ref, put)
    traffic.ready()
    dk_ref[...] = jnp.zeros(dk_ref.shape, f32)
    dv_ref[...] = jnp.zeros(dv_ref.shape, f32)

    def step(s):
        u, tile, block = key_step(s, low, high)
        queries = jnp.concatenate([qall_ref[block], daug[block, D:AUG, :]], axis=0)
        probs = jnp.exp(scores_of(kbd[u], queries, key_bias(u, tile, block, len_ref)))
        d_scores = probs * nn(vbd[u], daug[block])
        dv_ref[u] = dv_ref[u] + nt(probs.astype(bf16), daug[block])
        dk_ref[u] = dk_ref[u] + nt(d_scores.astype(bf16), queries)

    run_steps(step)
    unit = eye(D, D, f32)
    d_key = nt(unit, jnp.concatenate([own_heads(dk_ref[0]), own_heads(dk_ref[1])], axis=0), HIGH)
    d_value = nt(unit, jnp.concatenate([own_heads(dv_ref[0]), own_heads(dv_ref[1])], axis=0), HIGH)
    cosine, sine = own_rope(rope_ref, low, high)
    d_mixed = jnp.concatenate([dq_ref[...], rotate(d_key, cosine, -sine), d_value], axis=0).astype(bf16)
    d_in, d_gain = norm_back(resid_ref[...], gain_column(gains_ref, 2 * layer), nn(w_qkv_ref[layer], d_mixed))
    return grad_ref[...] + d_in, d_mixed, d_gain


def projection_grads(normal, d_mixed):
    tail = nt(normal, jnp.concatenate([d_mixed[MAXLAG:], jnp.zeros((TILE - 48, TILE), bf16)], axis=0))
    return nt(normal, d_mixed[:MAXLAG]), tail


def third_kernel(
    traffic, own_ref, other_ref, len_ref, qall_ref, kbd, vbd, dq_ref, grad_in_ref, resid_ref, att_ref, stat_ref, mid_ref, gate_up_ref,
    w_qkv_ref, w_out_ref, w_gate_up_ref, w_down_ref, gains_ref, rope_ref,
    copies_ref, grad_ref, payload_ref, d_mixed_ref, d_gain_a_ref, d_gain_b_ref, d_out_ref, d_gate_up_ref, d_branch_ref, hidden_ref,
    normal_b_ref,
    daug, dk_ref, dv_ref,
):
    grad, d_mixed_ref[...], d_gain_a_ref[...] = key_back(
        traffic, own_ref, other_ref, len_ref, qall_ref, kbd, vbd, dq_ref, grad_in_ref, resid_ref, 1, w_qkv_ref, gains_ref,
        rope_ref, daug, dk_ref, dv_ref,
    )
    low_refs = (d_out_ref, d_gate_up_ref, d_branch_ref, hidden_ref, normal_b_ref)
    grad, payload, d_gain_b_ref[...] = feed_back(
        grad, att_ref[...], mid_ref[...], gate_up_ref[...], w_out_ref[0], w_gate_up_ref[0], w_down_ref[0], gain_column(gains_ref, 1),
        stat_ref[...], low_refs, traffic,
    )
    grad_ref[...] = grad
    payload_ref[...] = payload
    copies_ref[...] = jnp.broadcast_to(payload[None], copies_ref.shape)


def second_window_kernel(
    traffic, len_ref, hidden_ref, d_out_ref, normal_ref, d_gate_up_ref, att_ref, d_branch_ref, d_gain_ref, payload_ref, q_ref, rope_ref,
    kaug_ref, vaug_ref, normal_all, w_qkv_ref,
    pack_ref, tail_ref, dq_ref, qall_ref, kbd, vbd, qbd, dbd, acc_ref,
):
    traffic.ready(8)
    tail = feed_grads(
        Tiles(pack_ref), hidden_ref[...], d_out_ref[...], normal_ref[...], d_gate_up_ref[...], att_ref[...], d_branch_ref[...]
    )
    tail_ref[...] = jnp.where(iota((1, TILE), 1) == 99, d_gain_ref[...], tail)
    traffic.send(pack_ref, tail_ref)
    query_back(
        traffic, 15, 1, payload_ref, q_ref, len_ref, rope_ref, kaug_ref, vaug_ref, normal_all, w_qkv_ref, dq_ref, qall_ref, kbd, vbd, qbd,
        dbd, acc_ref,
    )


def third_window_kernel(
    traffic, len_ref, pack_in_ref, tail_in_ref, normal_a_ref, d_mixed_ref, d_gain_a_ref, hidden_ref, d_out_ref, normal_ref, d_gate_up_ref,
    att_ref, d_branch_ref, d_gain_b_ref, payload_ref, q_ref, rope_ref, kaug_ref, vaug_ref, normal_all, w_qkv_ref,
    keep_ref, send_ref, rest_ref, tail0_ref, tail1_ref, dq_ref, qall_ref, kbd, vbd, qbd, dbd, acc_ref,
):
    traffic.ready(13)
    put = Pairs(lax.axis_index("tm") % 2, keep_ref, send_ref, rest_ref)
    for t in range(pack_in_ref.shape[0]):
        put.tile(pack_in_ref[t].astype(f32))
    head, tail = projection_grads(normal_a_ref[...], d_mixed_ref[...])
    put(head)
    tail0_ref[...] = feed_grads(
        put, hidden_ref[...], d_out_ref[...], normal_ref[...], d_gate_up_ref[...], att_ref[...], d_branch_ref[...]
    )
    lane = iota((1, TILE), 1)
    tail = jnp.where(lane == 98, d_gain_a_ref[...], tail + tail_in_ref[...])
    tail1_ref[...] = jnp.where(lane == 97, d_gain_b_ref[...], tail)
    traffic.send(keep_ref, send_ref, rest_ref, tail0_ref, tail1_ref)
    query_back(
        traffic, 20, 0, payload_ref, q_ref, len_ref, rope_ref, kaug_ref, vaug_ref, normal_all, w_qkv_ref, dq_ref, qall_ref, kbd, vbd, qbd,
        dbd, acc_ref,
    )


def last_kernel(
    traffic, own_ref, other_ref, len_ref, scale_ref, ids_ref, qall_ref, kbd, vbd, dq_ref, grad_in_ref, resid_ref, normal_a_ref, tail0_ref,
    tail1_ref, rest_ref, w_dense_ref, feats_ref, w_qkv_ref, gains_ref, rope_ref,
    keep_ref, send_ref, daug, dk_ref, dv_ref, raw_ref,
):
    chip, core, low, high = geometry()
    d_first, d_mixed, d_gain = key_back(
        traffic, own_ref, other_ref, len_ref, qall_ref, kbd, vbd, dq_ref, grad_in_ref, resid_ref, 0, w_qkv_ref, gains_ref,
        rope_ref, daug, dk_ref, dv_ref,
    )
    head, tail0 = projection_grads(normal_a_ref[...], d_mixed)
    d_first = d_first.astype(bf16)
    feats = feats_ref[...].astype(bf16)
    empty = jnp.zeros((64, TILE), bf16)
    tail0 = tail0 + tail0_ref[...] + nt(d_first, jnp.concatenate([empty, feats[:64]], axis=0))
    tail1 = tail1_ref[...] + nt(d_first, jnp.concatenate([empty, feats[64:], empty[:32]], axis=0))
    lane, row = iota((1, TILE), 1), iota((D, 1), 0)
    tail1 = jnp.where(lane == 96, d_gain, tail1)
    sums, counts = jnp.zeros((D, 1), f32), jnp.zeros((D, 1), f32)
    owner = (lax.axis_index("tm") == 0).astype(f32)
    for d in range(DOCS):
        hit = jnp.where(row == ids_ref[d], owner, 0.0)
        sums, counts = sums + hit * scale_ref[d], counts + hit
    high_part = sums.astype(bf16).astype(f32)
    tail1 = jnp.where(lane == 100, high_part, tail1)
    tail1 = jnp.where(lane == 101, sums - high_part, tail1)
    tail1 = jnp.where(lane == 102, counts, tail1)

    place = own_places(low, high)
    start = doc_start(place, len_ref)
    own = doc_scale_at(place, len_ref, scale_ref)
    flip = (iota((TILE, TILE), 0) + iota((TILE, TILE), 1) == TILE - 1).astype(bf16)
    raw_ref[...] = jnp.zeros(raw_ref.shape, f32)
    lags = TILE - iota((TILE, 1), 0)
    for b in range(3):
        weights = nn(w_dense_ref[:, b * TILE : (b + 1) * TILE], flip).astype(bf16)
        d_lagged = tn(weights, d_first)
        valid = place - (lags + b * TILE) >= start
        d_lagged = jnp.where(valid, d_lagged, 0.0) / own
        for u in range(2):
            half = jnp.where((lane < HALF) == (u == 0), d_lagged, 0.0)
            wide = jnp.concatenate([jnp.zeros((TILE, TILE), f32), half], axis=1)
            rolled = pltpu.roll(wide, TILE, 1, stride=1, stride_axis=0)
            total = jnp.sum(rolled, axis=0, keepdims=True)
            for tile, part in (((low if u == 0 else high) - b + 16, total[:, TILE:]), ((low if u == 0 else high) - b + 15, total[:, :TILE])):
                at = tile % 2, pl.ds(tile // 2, 1)
                raw_ref[at] = raw_ref[at] + part

    put = Pairs(core, keep_ref, send_ref)
    put.tile(rest_ref[0].astype(f32))
    for part in (head, tail0, tail1):
        put(part)
    for k in range(2):
        put.tile(raw_ref[k, 8:24, :])


def summed(in_ref):
    count, rows, _ = in_ref.shape
    total = jnp.zeros((rows, TILE), f32)
    return lax.fori_loop(0, count // 8, lambda i, t: t + jnp.sum(in_ref[pl.ds(i * 8, 8)].astype(f32), axis=0), total)


def pair_sum_kernel(early_ref, early_in_ref, late_ref, late_in_ref, out_ref):
    zero = jnp.zeros((16, TILE), bf16)
    late = late_ref.shape[0] - 1
    series = lax.axis_index("series")
    out_ref[:, 32:40, :] = jnp.zeros((64, 8, TILE), bf16)

    def both(ref, in_ref, t):
        return ref[t].astype(f32) + in_ref[t].astype(f32)

    for t in range(128):
        value = zero
        if t < EARLY:
            value = both(early_ref, early_in_ref, t).astype(bf16)
        elif t < EARLY + late:
            value = both(late_ref, late_in_ref, t - EARLY).astype(bf16)
        out_ref[t // 2, t % 2 * 16 : t % 2 * 16 + 16, :] = value
    raw = both(late_ref, late_in_ref, late)
    for c in range(16):
        line = jnp.where(iota((8, 1), 0) == 0, raw[c : c + 1], 0.0)
        out_ref[series * 16 + c, 32:40, :] = line.astype(bf16)


def sum_kernel(in_ref, out_ref, raw_ref):
    total = summed(in_ref)
    out_ref[...] = jnp.broadcast_to(total[:32].astype(bf16)[None], out_ref.shape)
    raw_ref[...] = total[32:33]


def unpack_kernel(own_ref, other_ref, lag_ref, qkv_ref, out_ref, gate_up_ref, down_ref, gains_ref, scale_ref):
    core = lax.axis_index("tm") % 2

    def tile(t):
        at = t // 4, slice(t // 2 % 2 * 16, t // 2 % 2 * 16 + 16)
        return jnp.where(core == t % 2, own_ref[at].astype(f32), other_ref[at].astype(f32))

    def columns(first, count):
        return [jnp.concatenate([tile(first + 9 * c + r) for r in range(9)], axis=0) for c in range(count)]

    layers = ((207, 234, 117), (90, 243, 0))
    tails = []
    for layer, (at_qkv, at_tail, at_rest) in enumerate(layers):
        for c, part in enumerate(columns(at_qkv, 3)):
            qkv_ref[layer, :, c * TILE : (c + 1) * TILE] = part
        tail = columns(at_tail, 1)[0]
        tails.append(tail)
        qkv_ref[layer, :, MAXLAG:] = tail[:, :48]
        for c, part in enumerate(columns(at_rest, 3)):
            down_ref[layer, :, c * TILE : (c + 1) * TILE] = part
        for c, part in enumerate(columns(at_rest + 27, 6)):
            gate_up_ref[layer, :, c * TILE : (c + 1) * TILE] = part
        out_ref[layer, :, :TILE] = columns(at_rest + 81, 1)[0]
        out_ref[layer, :, TILE:] = tail[:, 48:64]
    lag = jnp.where(iota((1, TILE), 1) < 64, pltpu.roll(tails[0], 64, 1), tails[1])
    lag_ref[...] = lag[:, :FEATS]
    pick = (iota((8, TILE), 1) == iota((8, TILE), 0) + 96).astype(bf16)
    rest = nt(pick, tails[1].astype(bf16))
    gains_ref[0] = rest[0:2]
    gains_ref[1] = rest[2:4]
    scale_ref[...] = ((rest[4:5] + rest[5:6]) / rest[6:7])[:, :DATASETS]


def weights_kernel(traffic, cot_ref, w_qkv_ref, w_out_ref, w_gate_up_ref, low_cot_ref, qkv_ref, out_ref, gate_up_ref):
    traffic.ready()
    low_cot_ref[...] = cot_ref[...].astype(bf16)
    for source, target in ((w_qkv_ref, qkv_ref), (w_out_ref, out_ref), (w_gate_up_ref, gate_up_ref)):
        for layer in range(LAYERS):
            target[layer] = turned(source[layer])


def first_values_kernel(traffic, raw_ref, hours_ref, out_ref):
    traffic.ready()
    both = jnp.concatenate([raw_ref[...], hours_ref[...].astype(f32)], axis=0)
    out_ref[...] = jnp.broadcast_to(both[None], out_ref.shape)


def shape(*dims, dtype=f32):
    return jax.ShapeDtypeStruct(dims, dtype)


class Traffic:
    def __init__(self, loads, stores):
        self.loads, self.stores, self.waited, self.sent = loads, stores, 0, set()
        for copy in loads:
            copy.start()

    def ready(self, count=None):
        count = len(self.loads) if count is None else count
        for copy in self.loads[self.waited : count]:
            copy.wait()
        self.waited = max(self.waited, count)

    def send(self, *refs):
        for ref, copy in self.stores:
            if any(ref is r for r in refs):
                copy.start()
                self.sent.add(id(copy))

    def finish(self):
        self.ready()
        for _, copy in self.stores:
            if id(copy) not in self.sent:
                copy.start()
        for _, copy in self.stores:
            copy.wait()


def call(kernel, operands, outs, scratch=(), tables=(), weights=(), cost=None):
    several = isinstance(outs, list)
    outs = outs if several else [outs]
    fetched = (*tables, *weights)
    buffers = [pltpu.SMEM(x.shape, x.dtype) for x in tables] + [pltpu.VMEM(x.shape, x.dtype) for x in weights]
    is_far = [not isinstance(out, jax.ShapeDtypeStruct) for out in outs]
    buffers += [pltpu.VMEM(out.shape, out.dtype) for out, far in zip(outs, is_far) if far]
    count, extra, copies = len(operands), len(buffers), len(buffers)

    def wrapped(*refs):
        refs = list(refs)
        ins, sources = refs[:count], refs[count : count + len(fetched)]
        results = refs[count + len(fetched) : count + len(fetched) + len(outs)]
        rest = refs[count + len(fetched) + len(outs) :]
        if not copies:
            kernel(*ins, *results, *rest)
            return
        own, held, sems = rest[: len(scratch)], rest[len(scratch) : -1], rest[-1]
        loads = [pltpu.make_async_copy(a, b, sems.at[n]) for n, (a, b) in enumerate(zip(sources, held))]
        stores, at = [], len(fetched)
        for n, far in enumerate(is_far):
            if far:
                stores.append((held[at], pltpu.make_async_copy(held[at], results[n], sems.at[at])))
                results[n] = held[at]
                at += 1
        traffic = Traffic(loads, stores)
        kernel(traffic, *ins, *held[: len(fetched)], *results, *own)
        traffic.finish()

    vmem, hbm = pl.BlockSpec(memory_space=pltpu.VMEM), pl.BlockSpec(memory_space=pltpu.HBM)
    results = pl.pallas_call(
        wrapped,
        out_shape=outs,
        in_specs=[vmem] * count + [hbm] * len(fetched),
        out_specs=[hbm if far else vmem for far in is_far],
        scratch_shapes=[*scratch, *buffers, pltpu.SemaphoreType.DMA((copies,))] if copies else list(scratch),
        compiler_params=pltpu.CompilerParams(vmem_limit_bytes=VMEM),
        cost_estimate=cost and pl.CostEstimate(flops=cost * 10**9, bytes_accessed=10**6, transcendentals=0),
    )(*operands, *(pltpu.with_memory_space_constraint(x, pltpu.HBM) for x in fetched))
    return results if several else results[0]


def pair_permute(x, bit):
    return lax.ppermute(x, "tm", [(i, i ^ bit) for i in range(32)])


def gather(copies, beside):
    groups = [[2 * chip + core for chip in range(16)] for core in range(2)]
    own = lax.all_to_all(copies, "tm", 0, 0, axis_index_groups=groups)
    own, beside = lax.optimization_barrier((own, beside))
    return own, pair_permute(own, 1), beside


def swap(block):
    return lax.ppermute(block, "tm", [(n, n if n % 2 == 0 else 32 - n) for n in range(32)])


def tile_halves(own, other):
    lane = iota((1, TILE), 1) < HALF
    return jnp.where(lane == (lax.axis_index("tm") < 16), own, other)


def rope_table():
    freqs = 10000.0 ** (-np.arange(8, dtype=np.float64) / 8)
    angle = np.arange(LEN, dtype=np.float64)[None, :] * freqs[:, None]
    return np.concatenate([np.cos(angle), np.sin(angle)], axis=0).astype(np.float32)


def body(
    raw_values, hours, doc_lengths, doc_scale, dataset_ids, lag_offsets, w_lag, w_qkv, w_out, w_gate_up, w_down, gains, cotangent
):
    lengths, scales, ids = doc_lengths.reshape(DOCS), doc_scale.reshape(DOCS), dataset_ids.reshape(DOCS)
    def low(*dims):
        return shape(*dims, dtype=bf16)

    def far(*dims, dtype=f32):
        return pltpu.HBM(dims, dtype)

    def far_low(*dims):
        return far(*dims, dtype=bf16)

    w_lag, w_down, lags = w_lag.T, w_down.transpose(0, 2, 1), lag_offsets.reshape(1, LAGS)
    rope = jnp.asarray(rope_table())
    values = lax.all_to_all(call(first_values_kernel, (), shape(32, 2, TILE), weights=(raw_values, hours)), "tm", 0, 0)
    aug, all_d = far_low(BLOCKS, AUG, BLOCK), far_low(BLOCKS, D, BLOCK)
    mine, mine_low, ff_low, column_shape = far(D, TILE), far_low(D, TILE), far_low(FF, TILE), far(D, 1)
    payload_shape = far_low(AUG, TILE)
    low_grads = [mine_low, far_low(2 * FF, TILE), mine_low, ff_low, mine_low]
    wide_bd = pltpu.VMEM((2, ROWS, WIDE), bf16)
    acc = pltpu.VMEM((2, ROWS, AUG), f32)
    top = pltpu.VMEM((2, ROWS, 1), f32)
    aug_scratch = pltpu.VMEM((BLOCKS, AUG, BLOCK), bf16)

    (copies, next1, resid1, kaug0, vaug0, normal_all0, lagged, feats, w_dense, resid0, normal_a0, q0, att0, stat0, mid0, gate_up0) = call(
        first_kernel,
        (values,),
        [low(16, D, TILE), mine_low, mine, aug, aug, all_d, far_low(LAGCOLS, TILE), far(96, TILE), far_low(D, LAGCOLS), mine, mine_low,
         far_low(TILE, D), mine_low, far_low(STAT, TILE), mine, far(2 * FF, TILE)],
        [pltpu.VMEM((8 + TILES, TILE), f32), pltpu.VMEM((TILE, MAXLAG + LEN), bf16), pltpu.VMEM((16, LEN), f32), wide_bd, top, acc],
        tables=(lengths, scales), weights=(lags, w_lag, w_qkv, w_out, w_gate_up, w_down, gains, rope),
    )

    low_cot, *turned_weights = call(
        weights_kernel, (), [mine_low, far_low(LAYERS, 3 * D, D), far_low(LAYERS, D, D), far_low(LAYERS, 2 * FF, D)],
        weights=(cotangent[0].T, w_qkv, w_out, w_gate_up),
    )
    own, other, cot = gather(copies, swap(low_cot))
    copies, act, kaug1, vaug1, normal_all1, q1, grad, payload, att1, d_gain_b1, *low1 = call(
        second_kernel,
        (own, other),
        [low(16, AUG, TILE), mine, aug, aug, all_d, far_low(TILE, D), mine, payload_shape, mine_low, column_shape, *low_grads],
        [wide_bd, top, acc],
        tables=(lengths,),
        weights=(cot, pair_permute(cot, 1), next1, resid1, *turned_weights, w_out, w_gate_up, w_down, gains, rope),
    )

    bd = pltpu.VMEM((2, ROWS, AUG), bf16)
    side_shapes = [mine, all_d, far_low(2, ROWS, WIDE), far_low(2, ROWS, AUG)]
    d_out, d_gate_up, d_branch, hidden, normal_b = low1
    pack, tail, dq, qall, kbd, vbd = call(
        second_window_kernel, (), [far_low(90, 16, TILE), mine, *side_shapes], [wide_bd, bd, acc],
        tables=(lengths,),
        weights=(hidden, d_out, normal_b, d_gate_up, att1, d_branch, d_gain_b1, payload, q1, rope, kaug1, vaug1, normal_all1,
                 turned_weights[0]), cost=8,
    )
    own, other, dq = gather(copies, dq)
    copies, grad, payload, d_mixed, d_gain_a1, d_gain_b0, *low0 = call(
        third_kernel,
        (own, other),
        [low(16, AUG, TILE), mine, payload_shape, far_low(3 * D, TILE), column_shape, column_shape, *low_grads],
        [aug_scratch, acc, acc],
        tables=(lengths,),
        weights=(qall, kbd, vbd, dq, grad, resid1, att0, stat0, mid0, gate_up0, w_qkv, w_out, w_gate_up, w_down, gains, rope),
    )
    d_out, d_gate_up, d_branch, hidden, normal_b = low0
    early, early_out, rest, tail0, tail1, dq, qall, kbd, vbd = call(
        third_window_kernel, (),
        [far_low(EARLY, 16, TILE), far_low(EARLY, 16, TILE), far_low(1, 16, TILE), mine, mine, *side_shapes], [wide_bd, bd, acc],
        tables=(lengths,),
        weights=(pack, tail, next1, d_mixed, d_gain_a1, hidden, d_out, normal_b, d_gate_up, att0, d_branch, d_gain_b0, payload, q0, rope,
                 kaug0, vaug0, normal_all0, turned_weights[0]), cost=8,
    )
    own, other, (dq, early_in) = gather(copies, (dq, pair_permute(early_out, 1)))
    late, late_out = call(
        last_kernel,
        (own, other),
        [low(LATE, 16, TILE)] * 2,
        [aug_scratch, acc, acc, pltpu.VMEM((2, 24, TILE), f32)],
        tables=(lengths, scales, ids),
        weights=(qall, kbd, vbd, dq, grad, resid0, normal_a0, tail0, tail1, rest, w_dense, feats, w_qkv, gains, rope),
    )
    packed = call(pair_sum_kernel, (early, early_in, late, pair_permute(late_out, 1)), low(64, 40, TILE))
    same_core = [[2 * chip + core for chip in range(64)] for core in range(2)]
    parts = lax.all_to_all(packed, ("series", "tm"), 0, 0, axis_index_groups=same_core)
    share, raw_grad = call(sum_kernel, (parts,), [low(64, 32, TILE), shape(1, TILE)])
    share, act = lax.optimization_barrier((share, act))
    own = lax.all_to_all(share, ("series", "tm"), 0, 0, axis_index_groups=same_core)
    own, act = lax.optimization_barrier((own, swap(tile_halves(act, pair_permute(act, 1)))))
    g_lag, g_qkv, g_out, g_gate_up, g_down, g_gains, scale = call(
        unpack_kernel,
        (own, pair_permute(own, 1)),
        [shape(D, FEATS), shape(LAYERS, D, 3 * D), shape(LAYERS, D, D), shape(LAYERS, D, 2 * FF), shape(LAYERS, D, FF),
         shape(LAYERS, 2, D), shape(1, DATASETS)],
    )
    return (
        act.T[None], raw_grad, scale.reshape(DATASETS), g_lag.T, g_qkv, g_out, g_gate_up, g_down.transpose(0, 2, 1), g_gains,
    )


def solution(mesh):
    placed = (
        P("series", "tm"),
        P("series", "tm"),
        P("series", None),
        P("series", None),
        P("series", None, None),
        P(),
        P(),
        P(),
        P(),
        P(),
        P(),
        P(),
        P("series", "tm", None),
    )
    return jax.shard_map(
        body,
        mesh=mesh,
        in_specs=placed,
        out_specs=(P("series", "tm", None), P("series", "tm"), P(), P(), P(), P(), P(), P(), P()),
        check_vma=False,
    )
```

profile of v0, /device:TPU:1, one launch (start us, length us, event | category | flops | bytes accessed | tf_op | source)
XLA Modules:
  0.0 171.5 jit_solution(3487821913576793165)
XLA Ops:
  1.3 16.7 %all_to_all.30.refs_0_ = f32[32,2,128]{2,1,0:T(2,128)S(1)} all-to-all(f32[32,2,128]{2,1,0:T(2,128)S(1)} %shard_map.205), channel_id=1, replica_groups=mesh['series'=4,'tm'=32] {'tm'}, dimensions={0} | all-to-all | bytes 65536 | tf_op jit(solution)/shard_map/all_to_all | solution.py:909
  18.0 12.7 %shard_map.206 = (bf16[16,144,128]{2,1,0:T(8,128)(2,1)}, bf16[144,128]{1,0:T(8,128)(2,1)}, f32[144,128]{1,0:T(8,128)}, bf16[8,192,512]{2,1,0:T(8,128)(2,1)}, bf1...) custom-call(f32[32,2,128]{2,1,0:T(2,128)S(1)} %all_to_all.30.refs_0_, ...), custom_call_target="tpu_custom_call" | custom-call | tf_op jit(solution)/shard_map/pallas_call | solution.py:856
  30.8 3.6 %all-to-all-start.1 = ((bf16[16,144,128]{2,1,0:T(8,128)(2,1)}), bf16[16,144,128]{2,1,0:T(8,128)(2,1)S(1)}, u32[]{:S(2)}, u32[]{:S(2)}) async-start(bf16[16,144,128]{2,1,0:T(8,128)(2,1)} %get-tuple-element.91), calls=%async_computation.1 | async-start | bytes 1179648 | tf_op jit(solution)/shard_map/all_to_all | solution.py:874
  34.4 2.9 %shard_map.207 = (bf16[144,128]{1,0:T(8,128)(2,1)}, bf16[2,432,144]{2,1,0:T(8,128)(2,1)}, bf16[2,144,144]{2,1,0:T(8,128)(2,1)}, bf16[2,768,144]{2,1,0:T(8,128)(2,1)}) custom-call(f32[144,128]{1,0:T(8,128)} %bitcast.19, bf16[2,144,432]{2,1,0:T(8,128)(2,1)} %refs_17_.3, bf16[2,144,144]{2,1,0:T(8,128)(2,1)} %refs_14_.2, bf16[2,144,768]{2,1,0:T(8,128)(2,1)} %refs_15_.2), custom_call_target="tpu_custom_call" | custom-call | tf_op jit(solution)/shard_map/pallas_call | solution.py:856
  37.3 6.6 %collective-permute-start = (bf16[144,128]{1,0:T(8,128)(2,1)}, bf16[144,128]{1,0:T(8,128)(2,1)S(1)}, u32[]{:S(2)}, u32[]{:S(2)}) collective-permute-start(bf16[144,128]{1,0:T(8,128)(2,1)} %get-tuple-element.92), channel_id=1, source_target_pairs={{0,0},{1,31},{2,2},{3,29},{4,4},{5,27},{6,6},{7,25},{8,8},{9,23},{... | collective-permute-start | bytes 110600 | tf_op jit(solution)/shard_map/ppermute | solution.py:880
  43.8 3.0 %collective-permute-done.refs_3_ = bf16[144,128]{1,0:T(8,128)(2,1)S(1)} collective-permute-done((bf16[144,128]{1,0:T(8,128)(2,1)}, bf16[144,128]{1,0:T(8,128)(2,1)S(1)}, u32[]{:S(2)}, u32[]{:S(2)}) %collective-permute-start) | collective-permute-done | bytes 36896 | tf_op jit(solution)/shard_map/ppermute | solution.py:880
  47.6 1.7 collective-permute-done.2.refs_4_
  49.9 11.1 %shard_map.208 = (bf16[16,192,128]{2,1,0:T(8,128)(2,1)}, f32[144,128]{1,0:T(8,128)}, bf16[8,192,512]{2,1,0:T(8,128)(2,1)}, bf16[8,192,512]{2,1,0:T(8,128)(2,1)},...) custom-call(bf16[16,144,128]{2,1,0:T(8,128)(2,1)S(1)} %all-to-all-do, ...), custom_call_target="tpu_custom_call" | custom-call | tf_op jit(solution)/shard_map/pallas_call | solution.py:856
  61.0 4.3 %all-to-all-start.2 = ((bf16[16,192,128]{2,1,0:T(8,128)(2,1)}), bf16[16,192,128]{2,1,0:T(8,128)(2,1)S(1)}, u32[]{:S(2)}, u32[]{:S(2)}) async-start(bf16[16,192,128]{2,1,0:T(8,128)(2,1)} %get-tuple-element.114), calls=%async_computation.2 | async-start | bytes 1572864 | tf_op jit(solution)/shard_map/all_to_all | solution.py:874
  65.4 10.2 %shard_map.209 = (bf16[90,16,128]{2,1,0:T(8,128)(2,1)}, f32[144,128]{1,0:T(8,128)}, f32[144,128]{1,0:T(8,128)}, bf16[8,144,512]{2,1,0:T(8,128)(2,1)}, bf16[2,576...) custom-call(s32[7]{0:T(128)} %bitcast.23, bf16[384,128]{1,0:T(8,128)(2,1)} %get-tuple-element.100.refs_1_, ...), custom_call_target="tpu_custom_call" | custom-call | flops 8000000000 | bytes 1000000 | tf_op jit(solution)/shard_map/pallas_call | solution.py:856
  75.6 3.5 %all-to-all-done.2.refs_0_ = bf16[16,192,128]{2,1,0:T(8,128)(2,1)S(1)} async-done(((bf16[16,192,128]{2,1,0:T(8,128)(2,1)}), bf16[16,192,128]{2,1,0:T(8,128)(2,1)S(1)}, u32[]{:S(2)}, u32[]{:S(2)}) %all-to-all-start.2) | async-done | bytes 786464 | tf_op jit(solution)/shard_map/all_to_all | solution.py:874
  79.1 1.6 collective-permute-start.3
  80.7 1.9 %collective-permute-done.3.refs_1_ = bf16[16,192,128]{2,1,0:T(8,128)(2,1)S(1)} collective-permute-done((bf16[16,192,128]{2,1,0:T(8,128)(2,1)S(1)}, bf16[16,192,128]{2,1,0:T(8,128)(2,1)S(1)}, u32[]{:S(2)}, u32[]{:S(2)}) %collective-permute-start.3) | collective-permute-done | bytes 786464 | tf_op jit(solution)/shard_map/ppermute | solution.py:869
  82.6 11.8 %shard_map.210 = (bf16[16,192,128]{2,1,0:T(8,128)(2,1)}, f32[144,128]{1,0:T(8,128)}, bf16[192,128]{1,0:T(8,128)(2,1)}, bf16[432,128]{1,0:T(8,128)(2,1)}, f32[144...) custom-call(bf16[16,192,128]{2,1,0:T(8,128)(2,1)S(1)} %all-to-all-do, ...), custom_call_target="tpu_custom_call" | custom-call | tf_op jit(solution)/shard_map/pallas_call | solution.py:856
  94.4 3.8 %all-to-all-start.3 = ((bf16[16,192,128]{2,1,0:T(8,128)(2,1)}), bf16[16,192,128]{2,1,0:T(8,128)(2,1)S(1)}, u32[]{:S(2)}, u32[]{:S(2)}) async-start(bf16[16,192,128]{2,1,0:T(8,128)(2,1)} %get-tuple-element.140), calls=%async_computation.3 | async-start | bytes 1572864 | tf_op jit(solution)/shard_map/all_to_all | solution.py:874
  98.2 10.6 %shard_map.211 = (bf16[103,16,128]{2,1,0:T(8,128)(2,1)}, bf16[103,16,128]{2,1,0:T(8,128)(2,1)}, bf16[1,16,128]{2,1,0:T(8,128)(2,1)}, f32[144,128]{1,0:T(8,128)},...) custom-call(s32[7]{0:T(128)} %bitcast.25, ...), custom_call_target="tpu_custom_call" | custom-call | flops 8000000000 | bytes 1000000 | tf_op jit(solution)/shard_map/pallas_call | solution.py:856
  109.3 1.6 collective-permute-done.4.refs_1_
  110.9 0.9 all-to-all-done.3.refs_0_
  111.8 1.5 collective-permute-start.5
  113.2 1.9 %collective-permute-done.5.refs_1_ = bf16[16,192,128]{2,1,0:T(8,128)(2,1)S(1)} collective-permute-done((bf16[16,192,128]{2,1,0:T(8,128)(2,1)S(1)}, bf16[16,192,128]{2,1,0:T(8,128)(2,1)S(1)}, u32[]{:S(2)}, u32[]{:S(2)}) %collective-permute-start.5) | collective-permute-done | bytes 786464 | tf_op jit(solution)/shard_map/ppermute | solution.py:869
  115.2 9.7 %shard_map.212 = (bf16[24,16,128]{2,1,0:T(8,128)(2,1)S(1)}, bf16[24,16,128]{2,1,0:T(8,128)(2,1)S(1)}) custom-call(bf16[16,192,128]{2,1,0:T(8,128)(2,1)S(1)} %all-to-all-done.3.refs_0_, bf16[16,192,128]{2,1,0:T(8,128)(2,1)S(1)} %collective-permute-done.5.refs_1_, s32[7]{0:T(128)} %bitcast.26, f32[7]{0:T(128)} %bitcast.28, s32[7]{0:T(128)} %bitcast.30, ...), custom_call_target="tpu_custom_call" | custom-call | tf_op jit(solution)/shard_map/pallas_call | solution.py:856
  125.3 0.9 collective-permute-done.6.refs_3_
  126.5 21.3 %all_to_all.31.refs_0_ = bf16[64,40,128]{2,1,0:T(8,128)(2,1)S(1)} all-to-all(bf16[64,40,128]{2,1,0:T(8,128)(2,1)S(1)} %shard_map.213), channel_id=1, replica_groups={{0,2,4,6,8,10,12,14,16,18,20,22,24,26,28,30,32,34,36,38,40,42,44,46,48,..., dimensions={0} | all-to-all | bytes 1310720 | tf_op jit(solution)/shard_map/all_to_all | solution.py:979
  147.8 0.9 shard_map.214
  148.7 5.0 %all-to-all-start.5 = ((bf16[64,32,128]{2,1,0:T(8,128)(2,1)}), bf16[64,32,128]{2,1,0:T(8,128)(2,1)S(1)}, u32[]{:S(2)}, u32[]{:S(2)}) async-start(bf16[64,32,128]{2,1,0:T(8,128)(2,1)} %get-tuple-element.161), calls=%async_computation.5 | async-start | bytes 1048576 | tf_op jit(solution)/shard_map/all_to_all | solution.py:982
  153.8 1.9 %collective-permute-start.7 = (f32[144,128]{1,0:T(8,128)S(1)}, f32[144,128]{1,0:T(8,128)S(1)}, u32[]{:S(2)}, u32[]{:S(2)}) collective-permute-start(f32[144,128]{1,0:T(8,128)S(1)} %copy-done.1), channel_id=1, source_target_pairs={{0,1},{1,0},{2,3},{3,2},{4,5},{5,4},{6,7},{7,6},{8,9},{9,8},{10,11... | collective-permute-start | bytes 221192 | tf_op jit(solution)/shard_map/ppermute | solution.py:869
  155.7 0.9 collective-permute-done.7
  156.6 6.5 %collective-permute-start.8 = (f32[144,128]{1,0:T(8,128)S(1)}, f32[144,128]{1,0:T(8,128)S(1)}, u32[]{:S(2)}, u32[]{:S(2)}) collective-permute-start(f32[144,128]{1,0:T(8,128)S(1)} %broadcast_select_fusion), channel_id=1, source_target_pairs={{0,0},{1,31},{2,2},{3,29},{4,4},{5,27},{6,6},{7,25},{8,8},{9,23},{... | collective-permute-start | bytes 221192 | tf_op jit(solution)/shard_map/ppermute | solution.py:880
  163.2 3.5 %collective-permute-done.8 = f32[144,128]{1,0:T(8,128)S(1)} collective-permute-done((f32[144,128]{1,0:T(8,128)S(1)}, f32[144,128]{1,0:T(8,128)S(1)}, u32[]{:S(2)}, u32[]{:S(2)}) %collective-permute-start.8) | collective-permute-done | bytes 73760 | tf_op jit(solution)/shard_map/ppermute | solution.py:880
  166.6 1.2 collective-permute-start.9
  167.8 1.5 collective-permute-done.9.refs_1_
  169.3 1.5 shard_map.215
  (20 shorter events, 3.8 us)
Async XLA Ops:
  30.8 16.1 %all-to-all-start.1 = ((bf16[16,144,128]{2,1,0:T(8,128)(2,1)}), bf16[16,144,128]{2,1,0:T(8,128)(2,1)S(1)}, u32[]{:S(2)}, u32[]{:S(2)}) async-start(bf16[16,144,128]{2,1,0:T(8,128)(2,1)} %get-tuple-element.91), calls=%async_computation.1 | async-start | bytes 1179648 | tf_op jit(solution)/shard_map/all_to_all | solution.py:874
  37.3 9.5 %collective-permute-start = (bf16[144,128]{1,0:T(8,128)(2,1)}, bf16[144,128]{1,0:T(8,128)(2,1)S(1)}, u32[]{:S(2)}, u32[]{:S(2)}) collective-permute-start(bf16[144,128]{1,0:T(8,128)(2,1)} %get-tuple-element.92), channel_id=1, source_target_pairs={{0,0},{1,31},{2,2},{3,29},{4,4},{5,27},{6,6},{7,25},{8,8},{9,23},{... | collective-permute-start | bytes 110600 | tf_op jit(solution)/shard_map/ppermute | solution.py:880
  46.8 2.5 %copy-start.2 = (bf16[144,128]{1,0:T(8,128)(2,1)}, bf16[144,128]{1,0:T(8,128)(2,1)S(1)}, u32[]{:S(2)}) copy-start(bf16[144,128]{1,0:T(8,128)(2,1)S(1)} %collective-permute-done.refs_3_) | copy-start | bytes 110596
  46.8 2.5 %collective-permute-start.1 = (bf16[16,144,128]{2,1,0:T(8,128)(2,1)S(1)}, bf16[16,144,128]{2,1,0:T(8,128)(2,1)S(1)}, u32[]{:S(2)}, u32[]{:S(2)}) collective-permute-start(bf16[16,144,128]{2,1,0:T(8,128)(2,1)S(1)} %all-to-all-done.1.refs_0_), channel_id=1, source_target_pairs={{0,1},{1,0},{2,3},{3,2},{4,5},{5,4},{6,7},{7,6},{8,9},{9,8},{10,11... | collective-permute-start | bytes 1769480 | tf_op jit(solution)/shard_map/ppermute | solution.py:869
  47.6 1.7 collective-permute-start.2
  49.3 0.6 copy-start.3
  61.0 18.1 %all-to-all-start.2 = ((bf16[16,192,128]{2,1,0:T(8,128)(2,1)}), bf16[16,192,128]{2,1,0:T(8,128)(2,1)S(1)}, u32[]{:S(2)}, u32[]{:S(2)}) async-start(bf16[16,192,128]{2,1,0:T(8,128)(2,1)} %get-tuple-element.114), calls=%async_computation.2 | async-start | bytes 1572864 | tf_op jit(solution)/shard_map/all_to_all | solution.py:874
  79.1 3.5 %collective-permute-start.3 = (bf16[16,192,128]{2,1,0:T(8,128)(2,1)S(1)}, bf16[16,192,128]{2,1,0:T(8,128)(2,1)S(1)}, u32[]{:S(2)}, u32[]{:S(2)}) collective-permute-start(bf16[16,192,128]{2,1,0:T(8,128)(2,1)S(1)} %all-to-all-done.2.refs_0_), channel_id=1, source_target_pairs={{0,1},{1,0},{2,3},{3,2},{4,5},{5,4},{6,7},{7,6},{8,9},{9,8},{10,11... | collective-permute-start | bytes 2359304 | tf_op jit(solution)/shard_map/ppermute | solution.py:869
  94.4 17.4 %all-to-all-start.3 = ((bf16[16,192,128]{2,1,0:T(8,128)(2,1)}), bf16[16,192,128]{2,1,0:T(8,128)(2,1)S(1)}, u32[]{:S(2)}, u32[]{:S(2)}) async-start(bf16[16,192,128]{2,1,0:T(8,128)(2,1)} %get-tuple-element.140), calls=%async_computation.3 | async-start | bytes 1572864 | tf_op jit(solution)/shard_map/all_to_all | solution.py:874
  108.8 2.1 %collective-permute-start.4 = (bf16[103,16,128]{2,1,0:T(8,128)(2,1)}, bf16[103,16,128]{2,1,0:T(8,128)(2,1)S(1)}, u32[]{:S(2)}, u32[]{:S(2)}) collective-permute-start(bf16[103,16,128]{2,1,0:T(8,128)(2,1)} %get-tuple-element.142), channel_id=1, source_target_pairs={{0,1},{1,0},{2,3},{3,2},{4,5},{5,4},{6,7},{7,6},{8,9},{9,8},{10,11... | collective-permute-start | bytes 1265672 | tf_op jit(solution)/shard_map/ppermute | solution.py:869
  111.8 3.4 %collective-permute-start.5 = (bf16[16,192,128]{2,1,0:T(8,128)(2,1)S(1)}, bf16[16,192,128]{2,1,0:T(8,128)(2,1)S(1)}, u32[]{:S(2)}, u32[]{:S(2)}) collective-permute-start(bf16[16,192,128]{2,1,0:T(8,128)(2,1)S(1)} %all-to-all-done.3.refs_0_), channel_id=1, source_target_pairs={{0,1},{1,0},{2,3},{3,2},{4,5},{5,4},{6,7},{7,6},{8,9},{9,8},{10,11... | collective-permute-start | bytes 2359304 | tf_op jit(solution)/shard_map/ppermute | solution.py:869
  115.2 11.1 %copy-start = (bf16[103,16,128]{2,1,0:T(8,128)(2,1)S(1)}, bf16[103,16,128]{2,1,0:T(8,128)(2,1)}, u32[]{:S(2)}) copy-start(bf16[103,16,128]{2,1,0:T(8,128)(2,1)} %get-tuple-element.139.refs_0_) | copy-start | bytes 1265668
  124.9 1.4 collective-permute-start.6
  126.4 27.3 %copy-start.1 = (f32[144,128]{1,0:T(8,128)S(1)}, f32[144,128]{1,0:T(8,128)}, u32[]{:S(2)}) copy-start(f32[144,128]{1,0:T(8,128)} %get-tuple-element.162) | copy-start | bytes 221188
  148.7 17.9 %all-to-all-start.5 = ((bf16[64,32,128]{2,1,0:T(8,128)(2,1)}), bf16[64,32,128]{2,1,0:T(8,128)(2,1)S(1)}, u32[]{:S(2)}, u32[]{:S(2)}) async-start(bf16[64,32,128]{2,1,0:T(8,128)(2,1)} %get-tuple-element.161), calls=%async_computation.5 | async-start | bytes 1048576 | tf_op jit(solution)/shard_map/all_to_all | solution.py:982
  153.8 2.9 %collective-permute-start.7 = (f32[144,128]{1,0:T(8,128)S(1)}, f32[144,128]{1,0:T(8,128)S(1)}, u32[]{:S(2)}, u32[]{:S(2)}) collective-permute-start(f32[144,128]{1,0:T(8,128)S(1)} %copy-done.1), channel_id=1, source_target_pairs={{0,1},{1,0},{2,3},{3,2},{4,5},{5,4},{6,7},{7,6},{8,9},{9,8},{10,11... | collective-permute-start | bytes 221192 | tf_op jit(solution)/shard_map/ppermute | solution.py:869
  156.6 10.0 %collective-permute-start.8 = (f32[144,128]{1,0:T(8,128)S(1)}, f32[144,128]{1,0:T(8,128)S(1)}, u32[]{:S(2)}, u32[]{:S(2)}) collective-permute-start(f32[144,128]{1,0:T(8,128)S(1)} %broadcast_select_fusion), channel_id=1, source_target_pairs={{0,0},{1,31},{2,2},{3,29},{4,4},{5,27},{6,6},{7,25},{8,8},{9,23},{... | collective-permute-start | bytes 221192 | tf_op jit(solution)/shard_map/ppermute | solution.py:880
  166.6 2.7 %collective-permute-start.9 = (bf16[64,32,128]{2,1,0:T(8,128)(2,1)S(1)}, bf16[64,32,128]{2,1,0:T(8,128)(2,1)S(1)}, u32[]{:S(2)}, u32[]{:S(2)}) collective-permute-start(bf16[64,32,128]{2,1,0:T(8,128)(2,1)S(1)} %all-to-all-done.5.refs_0_), channel_id=1, source_target_pairs={{0,1},{1,0},{2,3},{3,2},{4,5},{5,4},{6,7},{7,6},{8,9},{9,8},{10,11... | collective-permute-start | bytes 1572872 | tf_op jit(solution)/shard_map/ppermute | solution.py:869
where the time goes:
time: 172 us; the launch traced here: 171 us
  Pallas kernels  72.4 us (42%)
  blocking collectives  38 us (22%)
  starting transfers between devices  37.7 us (22%)
  waiting for transfers between devices  21.3 us (12%)
    pallas_call x11, Pallas kernels, call(): pl.pallas_call(wrapped, out_shape=outs, in_specs=[vmem] * count + [hbm] *...  72.4 us
    all_to_all x1, blocking collectives, body(): lax.all_to_all(packed, ('series', 'tm'), 0, 0, axis_index_groups=same_core)  21.3 us
    all_to_all x1, blocking collectives, body(): lax.all_to_all(call(first_values_kernel, (), shape(32, 2, TILE), weights=...  16.7 us
    ppermute x2, starting transfers between devices, swap(): lax.ppermute(block, 'tm', [(n, n if n % 2 == 0 else 32 - n) for n in rang...  13.1 us
    all_to_all x3, starting transfers between devices, gather(): own = lax.all_to_all(copies, 'tm', 0, 0, axis_index_groups=groups)  11.8 us
    ppermute x8, waiting for transfers between devices, pair_permute(): return lax.ppermute(x, 'tm', [(i, i ^ bit) for i in range(32)])  10.5 us
    ppermute x8, starting transfers between devices, pair_permute(): return lax.ppermute(x, 'tm', [(i, i ^ bit) for i in range(32)])  7.81 us
    ppermute x2, waiting for transfers between devices, swap(): lax.ppermute(block, 'tm', [(n, n if n % 2 == 0 else 32 - n) for n in rang...  6.42 us
  transfers between devices with their start and end apart: 14, of which 11 were waited for; matrix products, arithmetic and copies ran while one was open for 0% of the time, Pallas kernels for 14%

commit v1 on v0

--- a/solution.py
+++ b/solution.py
@@ -22,10 +22,10 @@
 FEATS = 87
 EPSILON = 1e-06
 MASKED = -1e30
-AUG = 192
+AUG = 176
 STAT = AUG - D
 LROW = D
-DROW = D + 27
+DROW = D + 18
 BLOCK = 512
 BLOCKS = LEN // BLOCK
 TILE = 128
@@ -160,11 +160,9 @@
     return total
 
 
-def three_parts(x):
+def two_parts(x):
     hi = x.astype(bf16)
-    rest = x - hi.astype(f32)
-    mid = rest.astype(bf16)
-    return hi, mid, (rest - mid.astype(f32)).astype(bf16)
+    return hi, (x - hi.astype(f32)).astype(bf16)
 
 
 class Tiles:
@@ -201,15 +199,16 @@
     return tn(w, eye(D, D, bf16)).astype(bf16)
 
 
-def key_value_block(normal, w_qkv, rope_ref, k, kaug_ref, vaug_ref):
+def with_ones(x):
+    return jnp.concatenate([x, jnp.ones((STAT, x.shape[1]), bf16)], axis=0)
+
+
+def key_value_block(normal, w_qkv, rope_ref, k, keys_ref, values_ref):
     mixed = nn(w_qkv[D:], normal)
     at = slice(k * BLOCK, (k + 1) * BLOCK)
     keys = rotate(mixed[:D], rope_ref[0:8, at], rope_ref[8:16, at])
-    ones = jnp.ones((STAT, BLOCK), bf16)
-    kaug_ref[k, 0:D, :] = keys.astype(bf16)
-    vaug_ref[k, 0:D, :] = mixed[D:].astype(bf16)
-    kaug_ref[k, D:AUG, :] = ones
-    vaug_ref[k, D:AUG, :] = ones
+    keys_ref[k] = keys.astype(bf16)
+    values_ref[k] = mixed[D:].astype(bf16)
     return head_sizes(keys)
 
 
@@ -230,7 +229,7 @@
     lane = iota((1, TILE), 1)
 
     def at(tile):
-        return ref[tile // 4, 0:D, pl.ds(pl.multiple_of((tile % 4) * TILE, TILE), TILE)].astype(f32)
+        return ref[tile // 4, :, pl.ds(pl.multiple_of((tile % 4) * TILE, TILE), TILE)].astype(f32)
 
     return jnp.where(lane < HALF, at(low), at(high)).astype(bf16)
 
@@ -279,7 +278,7 @@
     return jnp.max(jnp.sum((x * x).reshape(HEADS, HEAD_DIM, x.shape[1]), axis=1), axis=1, keepdims=True)
 
 
-def attend(query, k_size, kaug_ref, vaug_ref, len_ref, low, high, qbd, top_ref, acc_ref, q_rows_ref):
+def attend(query, k_size, keys_ref, values_ref, len_ref, low, high, qbd, top_ref, acc_ref, q_rows_ref):
     q_rows = nt(eye(TILE, TILE, bf16), query)
     q_rows_ref[...] = q_rows.astype(bf16)
     spread(qbd, jnp.concatenate([q_rows, jnp.zeros((TILE, STAT), f32)], axis=1))
@@ -293,8 +292,8 @@
 
         def step(s):
             u, tile, block = query_step(s, low, high)
-            scores = scores_of(qbd[u], kaug_ref[block], query_bias(u, tile, block, len_ref))
-            acc_ref[u] = acc_ref[u] + nt(jnp.exp(scores).astype(bf16), vaug_ref[block])
+            scores = scores_of(qbd[u], with_ones(keys_ref[block]), query_bias(u, tile, block, len_ref))
+            acc_ref[u] = acc_ref[u] + nt(jnp.exp(scores).astype(bf16), with_ones(values_ref[block]))
 
         run_steps(step)
 
@@ -304,11 +303,11 @@
 
         def step(s, carry):
             u, tile, block = query_step(s, low, high)
-            scores = scores_of(qbd[u], kaug_ref[block], query_bias(u, tile, block, len_ref))
+            scores = scores_of(qbd[u], with_ones(keys_ref[block]), query_bias(u, tile, block, len_ref))
             old = top_ref[u]
             new = jnp.maximum(old, jnp.max(scores, axis=1, keepdims=True))
             probs = jnp.exp(scores - new)
-            acc_ref[u] = acc_ref[u] * jnp.exp(old - new) + nt(probs.astype(bf16), vaug_ref[block])
+            acc_ref[u] = acc_ref[u] * jnp.exp(old - new) + nt(probs.astype(bf16), with_ones(values_ref[block]))
             top_ref[u] = new
             return carry
 
@@ -320,9 +319,9 @@
         acc = acc_ref[u]
         total = acc[:, D : D + 1]
         attended.append(own_heads(acc[:, :D] / total))
-        parts = three_parts(-(top_ref[u] + jnp.log(total)))
+        parts = two_parts(-(top_ref[u] + jnp.log(total)))
         stat = jnp.zeros((HALF, STAT), f32)
-        for j in range(3):
+        for j in range(2):
             part = parts[j].astype(f32)
             for h in range(HEADS):
                 stat = jnp.where(lane == 9 * j + h, part[h * HALF : (h + 1) * HALF], stat)
@@ -361,10 +360,8 @@
     product = d_att.astype(f32) * attended.astype(f32)
     delta = -jnp.sum(product.reshape(HEADS, HEAD_DIM, TILE), axis=1)
     delta = jnp.concatenate([delta, jnp.zeros((16 - HEADS, TILE), f32)], axis=0)
-    hi, lo, _ = three_parts(delta)
     row, col = iota((STAT, 16), 0), iota((STAT, 16), 1)
-    place = [((row == 27 + 9 * j + col) & (col < HEADS)).astype(bf16) for j in range(2)]
-    stat = stat.astype(f32) + nn(place[0], hi) + nn(place[1], lo)
+    stat = stat.astype(f32) + nn(((row == DROW - D + col) & (col < HEADS)).astype(bf16), delta.astype(bf16))
     return grad, jnp.concatenate([d_att, stat.astype(bf16)], axis=0), d_gain
 
 
@@ -381,17 +378,17 @@
 
 
 def first_kernel(
-    traffic, values_ref, len_ref, scale_ref, lag_ref, w_lag_ref, w_qkv_ref, w_out_ref, w_gate_up_ref, w_down_ref, gains_ref, rope_ref,
-    copies_ref, next_ref, next_resid_ref, kaug_ref, vaug_ref, normal_all, lagged_ref, feats_ref, w_dense_ref, resid_ref, normal_a_ref,
-    q_ref, att_ref, stat_ref, mid_ref, gate_up_ref,
+    traffic, raw_hours_ref, len_ref, scale_ref, lag_ref, w_lag_ref, gains_ref, w_qkv_ref, rope_ref, w_out_ref, w_gate_up_ref, w_down_ref,
+    copies_ref, next_ref, next_resid_ref, keys_ref, values_ref, normal_all, lagged_ref, feats_ref, w_dense_ref, resid_ref, normal_a_ref,
+    q_ref, att_ref, stat_ref, mid_ref, gate_up_ref, own_rope_ref,
     series, toeplitz, extra, qbd, top_ref, acc_ref,
 ):
     chip, core, low, high = geometry()
     traffic.ready(2)
     places = iota((TILES, TILE), 0) * TILE + iota((TILES, TILE), 1)
     own = doc_scale_at(places, len_ref, scale_ref)
-    values = values_ref[:, 0, :] / own
-    angle = values_ref[:, 1, :] * (2.0 * math.pi / 24.0)
+    values = raw_hours_ref[:, 0, :] / own
+    angle = raw_hours_ref[:, 1, :] * (2.0 * math.pi / 24.0)
     sine, cosine, level = jnp.sin(angle), jnp.cos(angle), jnp.log(own)
     series[0:8, :] = jnp.zeros((8, TILE), f32)
     series[8 : 8 + TILES, :] = values.astype(bf16).astype(f32)
@@ -411,7 +408,7 @@
 
     lax.fori_loop(0, TILES, shift, 0, unroll=4)
 
-    traffic.ready()
+    traffic.ready(7)
 
     rows = iota((FEATS, 1), 0)
     diagonal = iota((FEATS, LAGS), 0) == iota((FEATS, LAGS), 1)
@@ -422,7 +419,7 @@
     w_dense_ref[...] = w_dense
 
     gain_a, gain_b = gain_column(gains_ref, 0), gain_column(gains_ref, 1)
-    w_qkv = turned(w_qkv_ref[0])
+    w_qkv = turned(w_qkv_ref[...])
     lag_rows = iota((TILE, 1), 0) + 1
     k_size = jnp.zeros((HEADS, 1), f32)
     for k in range(BLOCKS):
@@ -440,9 +437,11 @@
         resid = nn(w_dense, jnp.concatenate(parts, axis=0))
         normal = (resid * norm_factor(resid) * gain_a).astype(bf16)
         normal_all[k] = normal
-        k_size = jnp.maximum(k_size, key_value_block(normal, w_qkv, rope_ref, k, kaug_ref, vaug_ref))
-
-    traffic.send(kaug_ref, vaug_ref, normal_all, w_dense_ref)
+        k_size = jnp.maximum(k_size, key_value_block(normal, w_qkv, rope_ref, k, keys_ref, values_ref))
+
+    cosine, sine = own_rope(rope_ref, low, high)
+    own_rope_ref[0:8], own_rope_ref[8:16] = cosine, sine
+    traffic.send(keys_ref, values_ref, normal_all, w_dense_ref, own_rope_ref)
 
     place = own_places(low, high)
     start = doc_start(place, len_ref)
@@ -464,12 +463,13 @@
     normal = (resid * norm_factor(resid) * gain_a).astype(bf16)
     normal_a_ref[...] = normal
     traffic.send(lagged_ref, feats_ref, resid_ref, normal_a_ref)
-    query = query_of(normal, w_qkv, *own_rope(rope_ref, low, high))
-    attended, stat_ref[...] = attend(query, k_size, kaug_ref, vaug_ref, len_ref, low, high, qbd, top_ref, acc_ref, q_ref)
+    query = query_of(normal, w_qkv, cosine, sine)
+    attended, stat_ref[...] = attend(query, k_size, keys_ref, values_ref, len_ref, low, high, qbd, top_ref, acc_ref, q_ref)
     att_ref[...] = attended
     traffic.send(q_ref, att_ref, stat_ref)
+    traffic.ready()
     mid, _, gate_up, _, resid = feed_forward(
-        resid, attended, turned(w_out_ref[0]), turned(w_gate_up_ref[0]), w_down_ref[0], gain_b
+        resid, attended, turned(w_out_ref[...]), turned(w_gate_up_ref[...]), w_down_ref[...], gain_b
     )
     mid_ref[...], gate_up_ref[...] = mid, gate_up
     traffic.send(mid_ref, gate_up_ref)
@@ -490,9 +490,9 @@
 
 
 def second_kernel(
-    traffic, own_ref, other_ref, len_ref, cot_own_ref, cot_other_ref, normal_ref, resid_in_ref, turned_qkv_ref, turned_out_ref,
-    turned_gate_up_ref, w_out_ref, w_gate_up_ref, w_down_ref, gains_ref, rope_ref,
-    copies_ref, act_ref, kaug_ref, vaug_ref, normal_all, q_ref, grad_ref, payload_ref, att_ref, d_gain_ref,
+    traffic, own_ref, other_ref, len_ref, turned_qkv_ref, rope_ref, normal_ref, own_rope_ref, cot_own_ref, cot_other_ref, resid_in_ref,
+    turned_out_ref, turned_gate_up_ref, w_out_ref, w_gate_up_ref, w_down_ref, gains_ref,
+    copies_ref, payload_ref, act_ref, keys_ref, values_ref, normal_all, q_ref, grad_ref, att_ref, d_gain_ref,
     d_out_ref, d_gate_up_ref, d_branch_ref, hidden_ref, normal_b_ref,
     qbd, top_ref, acc_ref,
 ):
@@ -503,18 +503,19 @@
 
     natural_tiles(own_ref, other_ref, put)
     traffic.send(normal_all)
-    traffic.ready()
-    w_qkv = turned_qkv_ref[1]
+    traffic.ready(5)
+    w_qkv = turned_qkv_ref[...]
     k_size = jnp.zeros((HEADS, 1), f32)
     for k in range(BLOCKS):
-        k_size = jnp.maximum(k_size, key_value_block(normal_all[k], w_qkv, rope_ref, k, kaug_ref, vaug_ref))
-    traffic.send(kaug_ref, vaug_ref)
-    query = query_of(normal_ref[...], w_qkv, *own_rope(rope_ref, low, high))
-    attended, stat = attend(query, k_size, kaug_ref, vaug_ref, len_ref, low, high, qbd, top_ref, acc_ref, q_ref)
+        k_size = jnp.maximum(k_size, key_value_block(normal_all[k], w_qkv, rope_ref, k, keys_ref, values_ref))
+    traffic.send(keys_ref, values_ref)
+    query = query_of(normal_ref[...], w_qkv, own_rope_ref[0:8], own_rope_ref[8:16])
+    attended, stat = attend(query, k_size, keys_ref, values_ref, len_ref, low, high, qbd, top_ref, acc_ref, q_ref)
+    traffic.ready()
     gain = gain_column(gains_ref, 3)
-    w_out, w_gate_up, w_down = w_out_ref[1], w_gate_up_ref[1], w_down_ref[1]
+    w_out, w_gate_up, w_down = w_out_ref[...], w_gate_up_ref[...], w_down_ref[...]
     mid, _, gate_up, _, out = feed_forward(
-        resid_in_ref[...], attended, turned_out_ref[1], turned_gate_up_ref[1], w_down, gain
+        resid_in_ref[...], attended, turned_out_ref[...], turned_gate_up_ref[...], w_down, gain
     )
     act_ref[...] = out
     att_ref[...] = attended
@@ -528,45 +529,53 @@
 
 
 def query_back(
-    traffic, count, layer, payload_ref, q_ref, len_ref, rope_ref, kaug_ref, vaug_ref, normal_all, w_qkv_ref, dq_ref, qall_ref, kbd, vbd,
-    qbd, dbd, acc_ref,
+    traffic, count, payload_ref, q_ref, len_ref, own_rope_ref, rope_ref, keys_ref, values_ref, normal_all, w_qkv_ref, dq_ref, qall_ref,
+    k_rows_ref, v_rows_ref, qbd, dbd, acc_ref,
 ):
     chip, core, low, high = geometry()
     traffic.ready(count)
     unit = eye(TILE, TILE, bf16)
     rows = nt(unit, payload_ref[...])
-    spread(qbd, jnp.concatenate([q_ref[...].astype(f32), rows[:, D:]], axis=1), LROW, LROW + 9, LROW + 18)
-    spread(dbd, rows, DROW, DROW + 9)
-    ones = jnp.ones((TILE, STAT), f32)
-    spread(kbd, jnp.concatenate([nt(unit, own_tile(kaug_ref, low, high)), ones], axis=1), LROW, LROW + 9, LROW + 18)
-    spread(vbd, jnp.concatenate([nt(unit, own_tile(vaug_ref, low, high)), ones], axis=1), DROW, DROW + 9)
-    w_qkv = w_qkv_ref[layer]
+    spread(qbd, jnp.concatenate([q_ref[...].astype(f32), rows[:, D:]], axis=1), LROW, LROW + 9)
+    spread(dbd, rows, DROW)
+    k_rows_ref[...] = nt(unit, own_tile(keys_ref, low, high)).astype(bf16)
+    v_rows_ref[...] = nt(unit, own_tile(values_ref, low, high)).astype(bf16)
+    w_qkv = w_qkv_ref[...]
     for k in range(BLOCKS):
         at = slice(k * BLOCK, (k + 1) * BLOCK)
         qall_ref[k] = query_of(normal_all[k], w_qkv, rope_ref[0:8, at], rope_ref[8:16, at])
-    traffic.send(kbd, vbd, qall_ref)
+    traffic.send(k_rows_ref, v_rows_ref, qall_ref)
     acc_ref[...] = jnp.zeros(acc_ref.shape, f32)
 
     def step(s):
         u, tile, block = query_step(s, low, high)
-        scores = scores_of(qbd[u], kaug_ref[block], query_bias(u, tile, block, len_ref))
-        d_scores = jnp.exp(scores) * nn(dbd[u], vaug_ref[block])
-        acc_ref[u] = acc_ref[u] + nt(d_scores.astype(bf16), kaug_ref[block])
+        scores = scores_of(qbd[u], with_ones(keys_ref[block]), query_bias(u, tile, block, len_ref))
+        d_scores = jnp.exp(scores) * nn(dbd[u], with_ones(values_ref[block]))
+        acc_ref[u] = acc_ref[u] + nt(d_scores.astype(bf16), keys_ref[block])
 
     run_steps(step)
     d_query = jnp.concatenate([own_heads(acc_ref[0]), own_heads(acc_ref[1])], axis=0) * HEAD_DIM**-0.5
-    cosine, sine = own_rope(rope_ref, low, high)
-    dq_ref[...] = rotate(nt(eye(D, D, f32), d_query, HIGH), cosine, -sine)
-
-
-def key_back(traffic, own_ref, other_ref, len_ref, qall_ref, kbd, vbd, dq_ref, grad_ref, resid_ref, layer, w_qkv_ref, gains_ref, rope_ref, daug, dk_ref, dv_ref):
+    dq_ref[...] = rotate(turned_rows(d_query), own_rope_ref[0:8], -own_rope_ref[8:16])
+
+
+def turned_rows(x):
+    hi, lo = two_parts(x)
+    unit = eye(D, D, bf16)
+    return nt(unit, hi) + nt(unit, lo)
+
+
+def key_back(traffic, count, own_ref, other_ref, len_ref, qall_ref, k_rows_ref, v_rows_ref, dq_ref, grad_ref, resid_ref, w_qkv_ref, gain,
+             own_rope_ref, daug, kbd, vbd, dk_ref, dv_ref):
     chip, core, low, high = geometry()
 
     def put(block, columns, value):
         daug[block, :, columns] = value
 
     natural_tiles(own_ref, other_ref, put)
-    traffic.ready()
+    traffic.ready(count)
+    ones = jnp.ones((TILE, STAT), f32)
+    spread(kbd, jnp.concatenate([k_rows_ref[...].astype(f32), ones], axis=1), LROW, LROW + 9)
+    spread(vbd, jnp.concatenate([v_rows_ref[...].astype(f32), ones], axis=1), DROW)
     dk_ref[...] = jnp.zeros(dk_ref.shape, f32)
     dv_ref[...] = jnp.zeros(dv_ref.shape, f32)
 
@@ -576,15 +585,15 @@
         probs = jnp.exp(scores_of(kbd[u], queries, key_bias(u, tile, block, len_ref)))
         d_scores = probs * nn(vbd[u], daug[block])
         dv_ref[u] = dv_ref[u] + nt(probs.astype(bf16), daug[block])
-        dk_ref[u] = dk_ref[u] + nt(d_scores.astype(bf16), queries)
+        dk_ref[u] = dk_ref[u] + nt(d_scores.astype(bf16), qall_ref[block])
 
     run_steps(step)
-    unit = eye(D, D, f32)
-    d_key = nt(unit, jnp.concatenate([own_heads(dk_ref[0]), own_heads(dk_ref[1])], axis=0), HIGH)
-    d_value = nt(unit, jnp.concatenate([own_heads(dv_ref[0]), own_heads(dv_ref[1])], axis=0), HIGH)
-    cosine, sine = own_rope(rope_ref, low, high)
-    d_mixed = jnp.concatenate([dq_ref[...], rotate(d_key, cosine, -sine), d_value], axis=0).astype(bf16)
-    d_in, d_gain = norm_back(resid_ref[...], gain_column(gains_ref, 2 * layer), nn(w_qkv_ref[layer], d_mixed))
+    traffic.ready()
+    d_key = turned_rows(jnp.concatenate([own_heads(dk_ref[0]), own_heads(dk_ref[1])], axis=0))
+    d_value = nt(eye(D, D, bf16), jnp.concatenate([own_heads(dv_ref[0]), own_heads(dv_ref[1])], axis=0).astype(bf16))
+    d_key = rotate(d_key, own_rope_ref[0:8], -own_rope_ref[8:16])
+    d_mixed = jnp.concatenate([dq_ref[...], d_key, d_value], axis=0).astype(bf16)
+    d_in, d_gain = norm_back(resid_ref[...], gain(), nn(w_qkv_ref[...], d_mixed))
     return grad_ref[...] + d_in, d_mixed, d_gain
 
 
@@ -594,19 +603,19 @@
 
 
 def third_kernel(
-    traffic, own_ref, other_ref, len_ref, qall_ref, kbd, vbd, dq_ref, grad_in_ref, resid_ref, att_ref, stat_ref, mid_ref, gate_up_ref,
-    w_qkv_ref, w_out_ref, w_gate_up_ref, w_down_ref, gains_ref, rope_ref,
-    copies_ref, grad_ref, payload_ref, d_mixed_ref, d_gain_a_ref, d_gain_b_ref, d_out_ref, d_gate_up_ref, d_branch_ref, hidden_ref,
+    traffic, own_ref, other_ref, len_ref, qall_ref, k_rows_ref, v_rows_ref, dq_ref, grad_in_ref, resid_ref, att_ref, stat_ref, mid_ref,
+    gate_up_ref, own_rope_ref, w_qkv_ref, w_out_ref, w_gate_up_ref, w_down_ref, gains_ref,
+    copies_ref, payload_ref, grad_ref, d_mixed_ref, d_gain_a_ref, d_gain_b_ref, d_out_ref, d_gate_up_ref, d_branch_ref, hidden_ref,
     normal_b_ref,
-    daug, dk_ref, dv_ref,
+    daug, kbd, vbd, dk_ref, dv_ref,
 ):
     grad, d_mixed_ref[...], d_gain_a_ref[...] = key_back(
-        traffic, own_ref, other_ref, len_ref, qall_ref, kbd, vbd, dq_ref, grad_in_ref, resid_ref, 1, w_qkv_ref, gains_ref,
-        rope_ref, daug, dk_ref, dv_ref,
+        traffic, 4, own_ref, other_ref, len_ref, qall_ref, k_rows_ref, v_rows_ref, dq_ref, grad_in_ref, resid_ref, w_qkv_ref,
+        lambda: gain_column(gains_ref, 2), own_rope_ref, daug, kbd, vbd, dk_ref, dv_ref,
     )
     low_refs = (d_out_ref, d_gate_up_ref, d_branch_ref, hidden_ref, normal_b_ref)
     grad, payload, d_gain_b_ref[...] = feed_back(
-        grad, att_ref[...], mid_ref[...], gate_up_ref[...], w_out_ref[0], w_gate_up_ref[0], w_down_ref[0], gain_column(gains_ref, 1),
+        grad, att_ref[...], mid_ref[...], gate_up_ref[...], w_out_ref[...], w_gate_up_ref[...], w_down_ref[...], gain_column(gains_ref, 1),
         stat_ref[...], low_refs, traffic,
     )
     grad_ref[...] = grad
@@ -615,9 +624,9 @@
 
 
 def second_window_kernel(
-    traffic, len_ref, hidden_ref, d_out_ref, normal_ref, d_gate_up_ref, att_ref, d_branch_ref, d_gain_ref, payload_ref, q_ref, rope_ref,
-    kaug_ref, vaug_ref, normal_all, w_qkv_ref,
-    pack_ref, tail_ref, dq_ref, qall_ref, kbd, vbd, qbd, dbd, acc_ref,
+    traffic, len_ref, hidden_ref, d_out_ref, normal_ref, d_gate_up_ref, att_ref, d_branch_ref, d_gain_ref, payload_ref, q_ref,
+    own_rope_ref, rope_ref, keys_ref, values_ref, normal_all, w_qkv_ref,
+    pack_ref, tail_ref, dq_ref, qall_ref, k_rows_ref, v_rows_ref, qbd, dbd, acc_ref,
 ):
     traffic.ready(8)
     tail = feed_grads(
@@ -626,15 +635,16 @@
     tail_ref[...] = jnp.where(iota((1, TILE), 1) == 99, d_gain_ref[...], tail)
     traffic.send(pack_ref, tail_ref)
     query_back(
-        traffic, 15, 1, payload_ref, q_ref, len_ref, rope_ref, kaug_ref, vaug_ref, normal_all, w_qkv_ref, dq_ref, qall_ref, kbd, vbd, qbd,
-        dbd, acc_ref,
+        traffic, 16, payload_ref, q_ref, len_ref, own_rope_ref, rope_ref, keys_ref, values_ref, normal_all, w_qkv_ref, dq_ref, qall_ref,
+        k_rows_ref, v_rows_ref, qbd, dbd, acc_ref,
     )
 
 
 def third_window_kernel(
     traffic, len_ref, pack_in_ref, tail_in_ref, normal_a_ref, d_mixed_ref, d_gain_a_ref, hidden_ref, d_out_ref, normal_ref, d_gate_up_ref,
-    att_ref, d_branch_ref, d_gain_b_ref, payload_ref, q_ref, rope_ref, kaug_ref, vaug_ref, normal_all, w_qkv_ref,
-    keep_ref, send_ref, rest_ref, tail0_ref, tail1_ref, dq_ref, qall_ref, kbd, vbd, qbd, dbd, acc_ref,
+    att_ref, d_branch_ref, d_gain_b_ref, payload_ref, q_ref, own_rope_ref, rope_ref, keys_ref, values_ref, normal_all,
+    w_qkv_ref,
+    keep_ref, send_ref, rest_ref, tail0_ref, tail1_ref, dq_ref, qall_ref, k_rows_ref, v_rows_ref, qbd, dbd, acc_ref,
 ):
     traffic.ready(13)
     put = Pairs(lax.axis_index("tm") % 2, keep_ref, send_ref, rest_ref)
@@ -650,20 +660,20 @@
     tail1_ref[...] = jnp.where(lane == 97, d_gain_b_ref[...], tail)
     traffic.send(keep_ref, send_ref, rest_ref, tail0_ref, tail1_ref)
     query_back(
-        traffic, 20, 0, payload_ref, q_ref, len_ref, rope_ref, kaug_ref, vaug_ref, normal_all, w_qkv_ref, dq_ref, qall_ref, kbd, vbd, qbd,
-        dbd, acc_ref,
+        traffic, 21, payload_ref, q_ref, len_ref, own_rope_ref, rope_ref, keys_ref, values_ref, normal_all, w_qkv_ref, dq_ref, qall_ref,
+        k_rows_ref, v_rows_ref, qbd, dbd, acc_ref,
     )
 
 
 def last_kernel(
-    traffic, own_ref, other_ref, len_ref, scale_ref, ids_ref, qall_ref, kbd, vbd, dq_ref, grad_in_ref, resid_ref, normal_a_ref, tail0_ref,
-    tail1_ref, rest_ref, w_dense_ref, feats_ref, w_qkv_ref, gains_ref, rope_ref,
-    keep_ref, send_ref, daug, dk_ref, dv_ref, raw_ref,
+    traffic, own_ref, other_ref, len_ref, scale_ref, ids_ref, qall_ref, k_rows_ref, v_rows_ref, dq_ref, grad_in_ref, resid_ref,
+    normal_a_ref, tail0_ref, tail1_ref, rest_ref, w_dense_ref, feats_ref, own_rope_ref, w_qkv_ref, gains_ref,
+    keep_ref, send_ref, daug, kbd, vbd, dk_ref, dv_ref, raw_ref,
 ):
     chip, core, low, high = geometry()
     d_first, d_mixed, d_gain = key_back(
-        traffic, own_ref, other_ref, len_ref, qall_ref, kbd, vbd, dq_ref, grad_in_ref, resid_ref, 0, w_qkv_ref, gains_ref,
-        rope_ref, daug, dk_ref, dv_ref,
+        traffic, 6, own_ref, other_ref, len_ref, qall_ref, k_rows_ref, v_rows_ref, dq_ref, grad_in_ref, resid_ref, w_qkv_ref,
+        lambda: gain_column(gains_ref, 0), own_rope_ref, daug, kbd, vbd, dk_ref, dv_ref,
     )
     head, tail0 = projection_grads(normal_a_ref[...], d_mixed)
     d_first = d_first.astype(bf16)
@@ -745,8 +755,9 @@
     raw_ref[...] = total[32:33]
 
 
-def unpack_kernel(own_ref, other_ref, lag_ref, qkv_ref, out_ref, gate_up_ref, down_ref, gains_ref, scale_ref):
+def unpack_kernel(own_ref, other_ref, act_in_ref, act_ref, lag_ref, qkv_ref, out_ref, gate_up_ref, down_ref, gains_ref, scale_ref):
     core = lax.axis_index("tm") % 2
+    act_ref[...] = act_in_ref[...]
 
     def tile(t):
         at = t // 4, slice(t // 2 % 2 * 16, t // 2 % 2 * 16 + 16)
@@ -778,12 +789,15 @@
     scale_ref[...] = ((rest[4:5] + rest[5:6]) / rest[6:7])[:, :DATASETS]
 
 
-def weights_kernel(traffic, cot_ref, w_qkv_ref, w_out_ref, w_gate_up_ref, low_cot_ref, qkv_ref, out_ref, gate_up_ref):
+def weights_kernel(traffic, cot_ref, w_qkv_ref, w_out_ref, w_gate_up_ref, low_cot_ref, qkv_ref, out_ref, gate_up_ref, first_qkv_ref):
+    traffic.ready(1)
+    low_cot_ref[...] = cot_ref[...].astype(bf16)
+    traffic.send(low_cot_ref)
     traffic.ready()
-    low_cot_ref[...] = cot_ref[...].astype(bf16)
-    for source, target in ((w_qkv_ref, qkv_ref), (w_out_ref, out_ref), (w_gate_up_ref, gate_up_ref)):
-        for layer in range(LAYERS):
-            target[layer] = turned(source[layer])
+    qkv_ref[...] = turned(w_qkv_ref[1])
+    first_qkv_ref[...] = turned(w_qkv_ref[0])
+    out_ref[...] = turned(w_out_ref[...])
+    gate_up_ref[...] = turned(w_gate_up_ref[...])
 
 
 def first_values_kernel(traffic, raw_ref, hours_ref, out_ref):
@@ -826,8 +840,10 @@
 def call(kernel, operands, outs, scratch=(), tables=(), weights=(), cost=None):
     several = isinstance(outs, list)
     outs = outs if several else [outs]
-    fetched = (*tables, *weights)
-    buffers = [pltpu.SMEM(x.shape, x.dtype) for x in tables] + [pltpu.VMEM(x.shape, x.dtype) for x in weights]
+    layers = [None] * len(tables) + [x[1] if isinstance(x, tuple) else None for x in weights]
+    fetched = (*tables, *(x[0] if isinstance(x, tuple) else x for x in weights))
+    shapes = [x.shape if layer is None else x.shape[1:] for x, layer in zip(fetched, layers)]
+    buffers = [(pltpu.SMEM if n < len(tables) else pltpu.VMEM)(shapes[n], x.dtype) for n, x in enumerate(fetched)]
     is_far = [not isinstance(out, jax.ShapeDtypeStruct) for out in outs]
     buffers += [pltpu.VMEM(out.shape, out.dtype) for out, far in zip(outs, is_far) if far]
     count, extra, copies = len(operands), len(buffers), len(buffers)
@@ -841,6 +857,7 @@
             kernel(*ins, *results, *rest)
             return
         own, held, sems = rest[: len(scratch)], rest[len(scratch) : -1], rest[-1]
+        sources = [a if layer is None else a.at[layer] for a, layer in zip(sources, layers)]
         loads = [pltpu.make_async_copy(a, b, sems.at[n]) for n, (a, b) in enumerate(zip(sources, held))]
         stores, at = [], len(fetched)
         for n, far in enumerate(is_far):
@@ -907,72 +924,75 @@
     w_lag, w_down, lags = w_lag.T, w_down.transpose(0, 2, 1), lag_offsets.reshape(1, LAGS)
     rope = jnp.asarray(rope_table())
     values = lax.all_to_all(call(first_values_kernel, (), shape(32, 2, TILE), weights=(raw_values, hours)), "tm", 0, 0)
-    aug, all_d = far_low(BLOCKS, AUG, BLOCK), far_low(BLOCKS, D, BLOCK)
+    all_d = far_low(BLOCKS, D, BLOCK)
     mine, mine_low, ff_low, column_shape = far(D, TILE), far_low(D, TILE), far_low(FF, TILE), far(D, 1)
-    payload_shape = far_low(AUG, TILE)
+    payload_shapes = [far_low(16, AUG, TILE), far_low(AUG, TILE)]
     low_grads = [mine_low, far_low(2 * FF, TILE), mine_low, ff_low, mine_low]
-    wide_bd = pltpu.VMEM((2, ROWS, WIDE), bf16)
-    acc = pltpu.VMEM((2, ROWS, AUG), f32)
+    bd, wide_bd = pltpu.VMEM((2, ROWS, AUG), bf16), pltpu.VMEM((2, ROWS, WIDE), bf16)
+    acc, acc_d = pltpu.VMEM((2, ROWS, AUG), f32), pltpu.VMEM((2, ROWS, D), f32)
     top = pltpu.VMEM((2, ROWS, 1), f32)
-    aug_scratch = pltpu.VMEM((BLOCKS, AUG, BLOCK), bf16)
-
-    (copies, next1, resid1, kaug0, vaug0, normal_all0, lagged, feats, w_dense, resid0, normal_a0, q0, att0, stat0, mid0, gate_up0) = call(
+    back_scratch = [pltpu.VMEM((BLOCKS, AUG, BLOCK), bf16), wide_bd, bd, acc_d, acc]
+
+    (copies, next1, resid1, keys0, values0, normal_all0, lagged, feats, w_dense, resid0, normal_a0, q0, att0, stat0, mid0, gate_up0,
+     own_rope) = call(
         first_kernel,
         (values,),
-        [low(16, D, TILE), mine_low, mine, aug, aug, all_d, far_low(LAGCOLS, TILE), far(96, TILE), far_low(D, LAGCOLS), mine, mine_low,
-         far_low(TILE, D), mine_low, far_low(STAT, TILE), mine, far(2 * FF, TILE)],
+        [far_low(16, D, TILE), mine_low, mine, all_d, all_d, all_d, far_low(LAGCOLS, TILE), far(96, TILE), far_low(D, LAGCOLS), mine,
+         mine_low, far_low(TILE, D), mine_low, far_low(STAT, TILE), mine, far(2 * FF, TILE), far(16, TILE)],
         [pltpu.VMEM((8 + TILES, TILE), f32), pltpu.VMEM((TILE, MAXLAG + LEN), bf16), pltpu.VMEM((16, LEN), f32), wide_bd, top, acc],
-        tables=(lengths, scales), weights=(lags, w_lag, w_qkv, w_out, w_gate_up, w_down, gains, rope),
-    )
-
-    low_cot, *turned_weights = call(
-        weights_kernel, (), [mine_low, far_low(LAYERS, 3 * D, D), far_low(LAYERS, D, D), far_low(LAYERS, 2 * FF, D)],
-        weights=(cotangent[0].T, w_qkv, w_out, w_gate_up),
+        tables=(lengths, scales), weights=(lags, w_lag, gains, (w_qkv, 0), rope, (w_out, 0), (w_gate_up, 0), (w_down, 0)),
+    )
+
+    low_cot, turned_qkv, turned_out, turned_gate_up, turned_qkv0 = call(
+        weights_kernel, (), [mine_low, far_low(3 * D, D), far_low(D, D), far_low(2 * FF, D), far_low(3 * D, D)],
+        weights=(cotangent[0].T, w_qkv, (w_out, 1), (w_gate_up, 1)),
     )
     own, other, cot = gather(copies, swap(low_cot))
-    copies, act, kaug1, vaug1, normal_all1, q1, grad, payload, att1, d_gain_b1, *low1 = call(
+    copies, payload, act, keys1, values1, normal_all1, q1, grad, att1, d_gain_b1, *low1 = call(
         second_kernel,
         (own, other),
-        [low(16, AUG, TILE), mine, aug, aug, all_d, far_low(TILE, D), mine, payload_shape, mine_low, column_shape, *low_grads],
+        [*payload_shapes, mine, all_d, all_d, all_d, far_low(TILE, D), mine, mine_low, column_shape, *low_grads],
         [wide_bd, top, acc],
         tables=(lengths,),
-        weights=(cot, pair_permute(cot, 1), next1, resid1, *turned_weights, w_out, w_gate_up, w_down, gains, rope),
-    )
-
-    bd = pltpu.VMEM((2, ROWS, AUG), bf16)
-    side_shapes = [mine, all_d, far_low(2, ROWS, WIDE), far_low(2, ROWS, AUG)]
+        weights=(turned_qkv, rope, next1, own_rope, cot, pair_permute(cot, 1), resid1, turned_out, turned_gate_up, (w_out, 1),
+                 (w_gate_up, 1), (w_down, 1), gains),
+    )
+
+    rows_low = far_low(TILE, D)
+    side_shapes = [mine, all_d, rows_low, rows_low]
     d_out, d_gate_up, d_branch, hidden, normal_b = low1
-    pack, tail, dq, qall, kbd, vbd = call(
-        second_window_kernel, (), [far_low(90, 16, TILE), mine, *side_shapes], [wide_bd, bd, acc],
+    pack, tail, dq, qall, k_rows, v_rows = call(
+        second_window_kernel, (), [far_low(90, 16, TILE), mine, *side_shapes], [wide_bd, bd, acc_d],
         tables=(lengths,),
-        weights=(hidden, d_out, normal_b, d_gate_up, att1, d_branch, d_gain_b1, payload, q1, rope, kaug1, vaug1, normal_all1,
-                 turned_weights[0]), cost=8,
+        weights=(hidden, d_out, normal_b, d_gate_up, att1, d_branch, d_gain_b1, payload, q1, own_rope, rope, keys1, values1, normal_all1,
+                 turned_qkv), cost=8,
     )
     own, other, dq = gather(copies, dq)
-    copies, grad, payload, d_mixed, d_gain_a1, d_gain_b0, *low0 = call(
+    copies, payload, grad, d_mixed, d_gain_a1, d_gain_b0, *low0 = call(
         third_kernel,
         (own, other),
-        [low(16, AUG, TILE), mine, payload_shape, far_low(3 * D, TILE), column_shape, column_shape, *low_grads],
-        [aug_scratch, acc, acc],
+        [*payload_shapes, mine, far_low(3 * D, TILE), column_shape, column_shape, *low_grads],
+        back_scratch,
         tables=(lengths,),
-        weights=(qall, kbd, vbd, dq, grad, resid1, att0, stat0, mid0, gate_up0, w_qkv, w_out, w_gate_up, w_down, gains, rope),
+        weights=(qall, k_rows, v_rows, dq, grad, resid1, att0, stat0, mid0, gate_up0, own_rope, (w_qkv, 1), (w_out, 0), (w_gate_up, 0),
+                 (w_down, 0), gains),
     )
     d_out, d_gate_up, d_branch, hidden, normal_b = low0
-    early, early_out, rest, tail0, tail1, dq, qall, kbd, vbd = call(
+    early, early_out, rest, tail0, tail1, dq, qall, k_rows, v_rows = call(
         third_window_kernel, (),
-        [far_low(EARLY, 16, TILE), far_low(EARLY, 16, TILE), far_low(1, 16, TILE), mine, mine, *side_shapes], [wide_bd, bd, acc],
+        [far_low(EARLY, 16, TILE), far_low(EARLY, 16, TILE), far_low(1, 16, TILE), mine, mine, *side_shapes], [wide_bd, bd, acc_d],
         tables=(lengths,),
-        weights=(pack, tail, next1, d_mixed, d_gain_a1, hidden, d_out, normal_b, d_gate_up, att0, d_branch, d_gain_b0, payload, q0, rope,
-                 kaug0, vaug0, normal_all0, turned_weights[0]), cost=8,
+        weights=(pack, tail, next1, d_mixed, d_gain_a1, hidden, d_out, normal_b, d_gate_up, att0, d_branch, d_gain_b0, payload, q0,
+                 own_rope, rope, keys0, values0, normal_all0, turned_qkv0), cost=8,
     )
     own, other, (dq, early_in) = gather(copies, (dq, pair_permute(early_out, 1)))
     late, late_out = call(
         last_kernel,
         (own, other),
         [low(LATE, 16, TILE)] * 2,
-        [aug_scratch, acc, acc, pltpu.VMEM((2, 24, TILE), f32)],
+        [*back_scratch, pltpu.VMEM((2, 24, TILE), f32)],
         tables=(lengths, scales, ids),
-        weights=(qall, kbd, vbd, dq, grad, resid0, normal_a0, tail0, tail1, rest, w_dense, feats, w_qkv, gains, rope),
+        weights=(qall, k_rows, v_rows, dq, grad, resid0, normal_a0, tail0, tail1, rest, w_dense, feats, own_rope, (w_qkv, 0), gains),
     )
     packed = call(pair_sum_kernel, (early, early_in, late, pair_permute(late_out, 1)), low(64, 40, TILE))
     same_core = [[2 * chip + core for chip in range(64)] for core in range(2)]
@@ -981,10 +1001,10 @@
     share, act = lax.optimization_barrier((share, act))
     own = lax.all_to_all(share, ("series", "tm"), 0, 0, axis_index_groups=same_core)
     own, act = lax.optimization_barrier((own, swap(tile_halves(act, pair_permute(act, 1)))))
-    g_lag, g_qkv, g_out, g_gate_up, g_down, g_gains, scale = call(
+    act, g_lag, g_qkv, g_out, g_gate_up, g_down, g_gains, scale = call(
         unpack_kernel,
-        (own, pair_permute(own, 1)),
-        [shape(D, FEATS), shape(LAYERS, D, 3 * D), shape(LAYERS, D, D), shape(LAYERS, D, 2 * FF), shape(LAYERS, D, FF),
+        (own, pair_permute(own, 1), act),
+        [shape(D, TILE), shape(D, FEATS), shape(LAYERS, D, 3 * D), shape(LAYERS, D, D), shape(LAYERS, D, 2 * FF), shape(LAYERS, D, FF),
          shape(LAYERS, 2, D), shape(1, DATASETS)],
     )
     return (

time: 172 us -> 165 us (0.959)
  Pallas kernels: 72.4 us -> 66.3 us
    pallas_call x11, Pallas kernels: 72.4 us -> 66.3 us  [call(): pl.pallas_call(wrapped, out_shape=outs, in_specs=[vmem] * count + [hbm] *...]
  transfers between devices with their start and end apart: 14 -> 14, of which waited for: 11 -> 11; matrix products, arithmetic and copies ran while one was open for 0% -> 0% of each run, Pallas kernels for 14% -> 13%
where the time goes in v1:
time: 165 us; the launch traced here: 164 us
  Pallas kernels  66.3 us (40%)
  blocking collectives  37.7 us (23%)
  starting transfers between devices  37.4 us (23%)
  waiting for transfers between devices  21.6 us (13%)
    pallas_call x11, Pallas kernels, call(): pl.pallas_call(wrapped, out_shape=outs, in_specs=[vmem] * count + [hbm] *...  66.3 us
    all_to_all x1, blocking collectives, body(): lax.all_to_all(packed, ('series', 'tm'), 0, 0, axis_index_groups=same_core)  21 us
    all_to_all x1, blocking collectives, body(): lax.all_to_all(call(first_values_kernel, (), shape(32, 2, TILE), weights=...  16.7 us
    ppermute x2, starting transfers between devices, swap(): lax.ppermute(block, 'tm', [(n, n if n % 2 == 0 else 32 - n) for n in rang...  13.1 us
    all_to_all x3, starting transfers between devices, gather(): own = lax.all_to_all(copies, 'tm', 0, 0, axis_index_groups=groups)  11.4 us
    ppermute x8, waiting for transfers between devices, pair_permute(): return lax.ppermute(x, 'tm', [(i, i ^ bit) for i in range(32)])  10.3 us
    ppermute x8, starting transfers between devices, pair_permute(): return lax.ppermute(x, 'tm', [(i, i ^ bit) for i in range(32)])  7.87 us
    ppermute x2, waiting for transfers between devices, swap(): lax.ppermute(block, 'tm', [(n, n if n % 2 == 0 else 32 - n) for n in rang...  6.82 us
  transfers between devices with their start and end apart: 14, of which 11 were waited for; matrix products, arithmetic and copies ran while one was open for 0% of the time, Pallas kernels for 13%

profile of v1, /device:TPU:1, one launch (start us, length us, event | category | flops | bytes accessed | tf_op | source)
XLA Modules:
  0.0 164.4 jit_solution(10057781644319670935)
XLA Ops:
  1.3 16.7 %all_to_all.30.refs_0_ = f32[32,2,128]{2,1,0:T(2,128)S(1)} all-to-all(f32[32,2,128]{2,1,0:T(2,128)S(1)} %shard_map.205), channel_id=1, replica_groups=mesh['series'=4,'tm'=32] {'tm'}, dimensions={0} | all-to-all | bytes 65536 | tf_op jit(solution)/shard_map/all_to_all | solution.py:926
  18.0 12.2 %shard_map.206 = (bf16[16,144,128]{2,1,0:T(8,128)(2,1)}, bf16[144,128]{1,0:T(8,128)(2,1)}, f32[144,128]{1,0:T(8,128)}, bf16[8,144,512]{2,1,0:T(8,128)(2,1)}, bf1...) custom-call(f32[32,2,128]{2,1,0:T(2,128)S(1)} %all_to_all.30.refs_0_, ...), custom_call_target="tpu_custom_call" | custom-call | tf_op jit(solution)/shard_map/pallas_call | solution.py:873
  30.2 3.6 %all-to-all-start.1 = ((bf16[16,144,128]{2,1,0:T(8,128)(2,1)}), bf16[16,144,128]{2,1,0:T(8,128)(2,1)S(1)}, u32[]{:S(2)}, u32[]{:S(2)}) async-start(bf16[16,144,128]{2,1,0:T(8,128)(2,1)} %get-tuple-element.94), calls=%async_computation.1 | async-start | bytes 1179648 | tf_op jit(solution)/shard_map/all_to_all | solution.py:891
  33.8 2.5 %shard_map.207 = (bf16[144,128]{1,0:T(8,128)(2,1)}, bf16[432,144]{1,0:T(8,128)(2,1)}, bf16[144,144]{1,0:T(8,128)(2,1)}, bf16[768,144]{1,0:T(8,128)(2,1)}, bf16[432,144]{1,0:T(8,128)(2,1)}) custom-call(f32[144,128]{1,0:T(8,128)} %bitcast.18, bf16[2,144,432]{2,1,0:T(8,128)(2,1)} %refs_18_.3, bf16[2,144,144]{2,1,0:T(8,128)(2,1)} %refs_15_.3, ...), custom_call_target="tpu_custom_call" | custom-call | tf_op jit(solution)/shard_map/pallas_call | solution.py:873
  36.4 6.6 %collective-permute-start = (bf16[144,128]{1,0:T(8,128)(2,1)}, bf16[144,128]{1,0:T(8,128)(2,1)S(1)}, u32[]{:S(2)}, u32[]{:S(2)}) collective-permute-start(bf16[144,128]{1,0:T(8,128)(2,1)} %get-tuple-element.95), channel_id=1, source_target_pairs={{0,0},{1,31},{2,2},{3,29},{4,4},{5,27},{6,6},{7,25},{8,8},{9,23},{... | collective-permute-start | bytes 110600 | tf_op jit(solution)/shard_map/ppermute | solution.py:897
  42.9 3.4 %collective-permute-done.refs_7_ = bf16[144,128]{1,0:T(8,128)(2,1)S(1)} collective-permute-done((bf16[144,128]{1,0:T(8,128)(2,1)}, bf16[144,128]{1,0:T(8,128)(2,1)S(1)}, u32[]{:S(2)}, u32[]{:S(2)}) %collective-permute-start) | collective-permute-done | bytes 36896 | tf_op jit(solution)/shard_map/ppermute | solution.py:897
  47.1 1.7 %collective-permute-done.2.refs_8_ = bf16[144,128]{1,0:T(8,128)(2,1)S(1)} collective-permute-done((bf16[144,128]{1,0:T(8,128)(2,1)S(1)}, bf16[144,128]{1,0:T(8,128)(2,1)S(1)}, u32[]{:S(2)}, u32[]{:S(2)}) %collective-permute-start.2) | collective-permute-done | bytes 36896 | tf_op jit(solution)/shard_map/ppermute | solution.py:886
  49.4 9.4 %shard_map.208 = (bf16[16,176,128]{2,1,0:T(8,128)(2,1)}, bf16[176,128]{1,0:T(8,128)(2,1)}, f32[144,128]{1,0:T(8,128)}, bf16[8,144,512]{2,1,0:T(8,128)(2,1)}, bf1...) custom-call(bf16[16,144,128]{2,1,0:T(8,128)(2,1)S(1)} %all-to-all-do, ...), custom_call_target="tpu_custom_call" | custom-call | tf_op jit(solution)/shard_map/pallas_call | solution.py:873
  58.8 4.0 %all-to-all-start.2 = ((bf16[16,176,128]{2,1,0:T(8,128)(2,1)}), bf16[16,176,128]{2,1,0:T(8,128)(2,1)S(1)}, u32[]{:S(2)}, u32[]{:S(2)}) async-start(bf16[16,176,128]{2,1,0:T(8,128)(2,1)} %get-tuple-element.118), calls=%async_computation.2 | async-start | bytes 1441792 | tf_op jit(solution)/shard_map/all_to_all | solution.py:891
  62.8 9.6 %shard_map.209 = (bf16[90,16,128]{2,1,0:T(8,128)(2,1)}, f32[144,128]{1,0:T(8,128)}, f32[144,128]{1,0:T(8,128)}, bf16[8,144,512]{2,1,0:T(8,128)(2,1)}, bf16[128,1...) custom-call(s32[7]{0:T(128)} %bitcast.22, bf16[384,128]{1,0:T(8,128)(2,1)} %get-tuple-element.104.refs_1_, ...), custom_call_target="tpu_custom_call" | custom-call | flops 8000000000 | bytes 1000000 | tf_op jit(solution)/shard_map/pallas_call | solution.py:873
  72.4 3.4 %all-to-all-done.2.refs_0_ = bf16[16,176,128]{2,1,0:T(8,128)(2,1)S(1)} async-done(((bf16[16,176,128]{2,1,0:T(8,128)(2,1)}), bf16[16,176,128]{2,1,0:T(8,128)(2,1)S(1)}, u32[]{:S(2)}, u32[]{:S(2)}) %all-to-all-start.2) | async-done | bytes 720928 | tf_op jit(solution)/shard_map/all_to_all | solution.py:891
  75.8 1.6 collective-permute-start.3
  77.4 1.8 %collective-permute-done.3.refs_1_ = bf16[16,176,128]{2,1,0:T(8,128)(2,1)S(1)} collective-permute-done((bf16[16,176,128]{2,1,0:T(8,128)(2,1)S(1)}, bf16[16,176,128]{2,1,0:T(8,128)(2,1)S(1)}, u32[]{:S(2)}, u32[]{:S(2)}) %collective-permute-start.3) | collective-permute-done | bytes 720928 | tf_op jit(solution)/shard_map/ppermute | solution.py:886
  79.2 10.1 %shard_map.210 = (bf16[16,176,128]{2,1,0:T(8,128)(2,1)}, bf16[176,128]{1,0:T(8,128)(2,1)}, f32[144,128]{1,0:T(8,128)}, bf16[432,128]{1,0:T(8,128)(2,1)}, f32[144...) custom-call(bf16[16,176,128]{2,1,0:T(8,128)(2,1)S(1)} %all-to-all-do, ...), custom_call_target="tpu_custom_call" | custom-call | tf_op jit(solution)/shard_map/pallas_call | solution.py:873
  89.3 3.8 %all-to-all-start.3 = ((bf16[16,176,128]{2,1,0:T(8,128)(2,1)}), bf16[16,176,128]{2,1,0:T(8,128)(2,1)S(1)}, u32[]{:S(2)}, u32[]{:S(2)}) async-start(bf16[16,176,128]{2,1,0:T(8,128)(2,1)} %get-tuple-element.145), calls=%async_computation.3 | async-start | bytes 1441792 | tf_op jit(solution)/shard_map/all_to_all | solution.py:891
  93.2 9.7 %shard_map.211 = (bf16[103,16,128]{2,1,0:T(8,128)(2,1)}, bf16[103,16,128]{2,1,0:T(8,128)(2,1)}, bf16[1,16,128]{2,1,0:T(8,128)(2,1)}, f32[144,128]{1,0:T(8,128)},...) custom-call(s32[7]{0:T(128)} %bitcast.24, ...), custom_call_target="tpu_custom_call" | custom-call | flops 8000000000 | bytes 1000000 | tf_op jit(solution)/shard_map/pallas_call | solution.py:873
  103.3 1.6 collective-permute-done.4.refs_1_
  104.9 1.1 all-to-all-done.3.refs_0_
  106.0 1.5 collective-permute-start.5
  107.5 1.8 %collective-permute-done.5.refs_1_ = bf16[16,176,128]{2,1,0:T(8,128)(2,1)S(1)} collective-permute-done((bf16[16,176,128]{2,1,0:T(8,128)(2,1)S(1)}, bf16[16,176,128]{2,1,0:T(8,128)(2,1)S(1)}, u32[]{:S(2)}, u32[]{:S(2)}) %collective-permute-start.5) | collective-permute-done | bytes 720928 | tf_op jit(solution)/shard_map/ppermute | solution.py:886
  109.3 9.4 %shard_map.212 = (bf16[24,16,128]{2,1,0:T(8,128)(2,1)S(1)}, bf16[24,16,128]{2,1,0:T(8,128)(2,1)S(1)}) custom-call(bf16[16,176,128]{2,1,0:T(8,128)(2,1)S(1)} %all-to-all-done.3.refs_0_, bf16[16,176,128]{2,1,0:T(8,128)(2,1)S(1)} %collective-permute-done.5.refs_1_, s32[7]{0:T(128)} %bitcast.25, f32[7]{0:T(128)} %bitcast.27, s32[7]{0:T(128)} %bitcast.29, ...), custom_call_target="tpu_custom_call" | custom-call | tf_op jit(solution)/shard_map/pallas_call | solution.py:873
  119.2 0.9 collective-permute-done.6.refs_3_
  120.3 21.0 %all_to_all.31.refs_0_ = bf16[64,40,128]{2,1,0:T(8,128)(2,1)S(1)} all-to-all(bf16[64,40,128]{2,1,0:T(8,128)(2,1)S(1)} %shard_map.213), channel_id=1, replica_groups={{0,2,4,6,8,10,12,14,16,18,20,22,24,26,28,30,32,34,36,38,40,42,44,46,48,..., dimensions={0} | all-to-all | bytes 1310720 | tf_op jit(solution)/shard_map/all_to_all | solution.py:999
  141.3 0.9 shard_map.214
  142.2 5.0 %all-to-all-start.5 = ((bf16[64,32,128]{2,1,0:T(8,128)(2,1)}), bf16[64,32,128]{2,1,0:T(8,128)(2,1)S(1)}, u32[]{:S(2)}, u32[]{:S(2)}) async-start(bf16[64,32,128]{2,1,0:T(8,128)(2,1)} %get-tuple-element.166), calls=%async_computation.5 | async-start | bytes 1048576 | tf_op jit(solution)/shard_map/all_to_all | solution.py:1002
  147.3 1.9 %collective-permute-start.7 = (f32[144,128]{1,0:T(8,128)S(1)}, f32[144,128]{1,0:T(8,128)S(1)}, u32[]{:S(2)}, u32[]{:S(2)}) collective-permute-start(f32[144,128]{1,0:T(8,128)S(1)} %copy-done.1), channel_id=1, source_target_pairs={{0,1},{1,0},{2,3},{3,2},{4,5},{5,4},{6,7},{7,6},{8,9},{9,8},{10,11... | collective-permute-start | bytes 221192 | tf_op jit(solution)/shard_map/ppermute | solution.py:886
  149.2 0.9 collective-permute-done.7
  150.1 6.5 %collective-permute-start.8 = (f32[144,128]{1,0:T(8,128)S(1)}, f32[144,128]{1,0:T(8,128)S(1)}, u32[]{:S(2)}, u32[]{:S(2)}) collective-permute-start(f32[144,128]{1,0:T(8,128)S(1)} %broadcast_select_fusion), channel_id=1, source_target_pairs={{0,0},{1,31},{2,2},{3,29},{4,4},{5,27},{6,6},{7,25},{8,8},{9,23},{... | collective-permute-start | bytes 221192 | tf_op jit(solution)/shard_map/ppermute | solution.py:897
  156.7 3.5 %collective-permute-done.8.refs_2_ = f32[144,128]{1,0:T(8,128)S(1)} collective-permute-done((f32[144,128]{1,0:T(8,128)S(1)}, f32[144,128]{1,0:T(8,128)S(1)}, u32[]{:S(2)}, u32[]{:S(2)}) %collective-permute-start.8) | collective-permute-done | bytes 73760 | tf_op jit(solution)/shard_map/ppermute | solution.py:897
  160.1 1.2 collective-permute-start.9
  161.3 1.5 collective-permute-done.9.refs_1_
  162.8 1.5 shard_map.215
  (19 shorter events, 3.2 us)
Async XLA Ops:
  30.2 16.1 %all-to-all-start.1 = ((bf16[16,144,128]{2,1,0:T(8,128)(2,1)}), bf16[16,144,128]{2,1,0:T(8,128)(2,1)S(1)}, u32[]{:S(2)}, u32[]{:S(2)}) async-start(bf16[16,144,128]{2,1,0:T(8,128)(2,1)} %get-tuple-element.94), calls=%async_computation.1 | async-start | bytes 1179648 | tf_op jit(solution)/shard_map/all_to_all | solution.py:891
  36.4 9.9 %collective-permute-start = (bf16[144,128]{1,0:T(8,128)(2,1)}, bf16[144,128]{1,0:T(8,128)(2,1)S(1)}, u32[]{:S(2)}, u32[]{:S(2)}) collective-permute-start(bf16[144,128]{1,0:T(8,128)(2,1)} %get-tuple-element.95), channel_id=1, source_target_pairs={{0,0},{1,31},{2,2},{3,29},{4,4},{5,27},{6,6},{7,25},{8,8},{9,23},{... | collective-permute-start | bytes 110600 | tf_op jit(solution)/shard_map/ppermute | solution.py:897
  46.3 2.5 %copy-start.2 = (bf16[144,128]{1,0:T(8,128)(2,1)}, bf16[144,128]{1,0:T(8,128)(2,1)S(1)}, u32[]{:S(2)}) copy-start(bf16[144,128]{1,0:T(8,128)(2,1)S(1)} %collective-permute-done.refs_7_) | copy-start | bytes 110596
  46.3 2.5 %collective-permute-start.1 = (bf16[16,144,128]{2,1,0:T(8,128)(2,1)S(1)}, bf16[16,144,128]{2,1,0:T(8,128)(2,1)S(1)}, u32[]{:S(2)}, u32[]{:S(2)}) collective-permute-start(bf16[16,144,128]{2,1,0:T(8,128)(2,1)S(1)} %all-to-all-done.1.refs_0_), channel_id=1, source_target_pairs={{0,1},{1,0},{2,3},{3,2},{4,5},{5,4},{6,7},{7,6},{8,9},{9,8},{10,11... | collective-permute-start | bytes 1769480 | tf_op jit(solution)/shard_map/ppermute | solution.py:886
  47.1 1.7 %collective-permute-start.2 = (bf16[144,128]{1,0:T(8,128)(2,1)S(1)}, bf16[144,128]{1,0:T(8,128)(2,1)S(1)}, u32[]{:S(2)}, u32[]{:S(2)}) collective-permute-start(bf16[144,128]{1,0:T(8,128)(2,1)S(1)} %collective-permute-done.refs_7_), channel_id=1, source_target_pairs={{0,1},{1,0},{2,3},{3,2},{4,5},{5,4},{6,7},{7,6},{8,9},{9,8},{10,11... | collective-permute-start | bytes 110600 | tf_op jit(solution)/shard_map/ppermute | solution.py:886
  48.7 0.6 copy-start.3
  58.8 17.0 %all-to-all-start.2 = ((bf16[16,176,128]{2,1,0:T(8,128)(2,1)}), bf16[16,176,128]{2,1,0:T(8,128)(2,1)S(1)}, u32[]{:S(2)}, u32[]{:S(2)}) async-start(bf16[16,176,128]{2,1,0:T(8,128)(2,1)} %get-tuple-element.118), calls=%async_computation.2 | async-start | bytes 1441792 | tf_op jit(solution)/shard_map/all_to_all | solution.py:891
  75.8 3.4 %collective-permute-start.3 = (bf16[16,176,128]{2,1,0:T(8,128)(2,1)S(1)}, bf16[16,176,128]{2,1,0:T(8,128)(2,1)S(1)}, u32[]{:S(2)}, u32[]{:S(2)}) collective-permute-start(bf16[16,176,128]{2,1,0:T(8,128)(2,1)S(1)} %all-to-all-done.2.refs_0_), channel_id=1, source_target_pairs={{0,1},{1,0},{2,3},{3,2},{4,5},{5,4},{6,7},{7,6},{8,9},{9,8},{10,11... | collective-permute-start | bytes 2162696 | tf_op jit(solution)/shard_map/ppermute | solution.py:886
  89.3 16.7 %all-to-all-start.3 = ((bf16[16,176,128]{2,1,0:T(8,128)(2,1)}), bf16[16,176,128]{2,1,0:T(8,128)(2,1)S(1)}, u32[]{:S(2)}, u32[]{:S(2)}) async-start(bf16[16,176,128]{2,1,0:T(8,128)(2,1)} %get-tuple-element.145), calls=%async_computation.3 | async-start | bytes 1441792 | tf_op jit(solution)/shard_map/all_to_all | solution.py:891
  102.9 2.1 %collective-permute-start.4 = (bf16[103,16,128]{2,1,0:T(8,128)(2,1)}, bf16[103,16,128]{2,1,0:T(8,128)(2,1)S(1)}, u32[]{:S(2)}, u32[]{:S(2)}) collective-permute-start(bf16[103,16,128]{2,1,0:T(8,128)(2,1)} %get-tuple-element.147), channel_id=1, source_target_pairs={{0,1},{1,0},{2,3},{3,2},{4,5},{5,4},{6,7},{7,6},{8,9},{9,8},{10,11... | collective-permute-start | bytes 1265672 | tf_op jit(solution)/shard_map/ppermute | solution.py:886
  106.0 3.3 %collective-permute-start.5 = (bf16[16,176,128]{2,1,0:T(8,128)(2,1)S(1)}, bf16[16,176,128]{2,1,0:T(8,128)(2,1)S(1)}, u32[]{:S(2)}, u32[]{:S(2)}) collective-permute-start(bf16[16,176,128]{2,1,0:T(8,128)(2,1)S(1)} %all-to-all-done.3.refs_0_), channel_id=1, source_target_pairs={{0,1},{1,0},{2,3},{3,2},{4,5},{5,4},{6,7},{7,6},{8,9},{9,8},{10,11... | collective-permute-start | bytes 2162696 | tf_op jit(solution)/shard_map/ppermute | solution.py:886
  109.3 10.8 %copy-start = (bf16[103,16,128]{2,1,0:T(8,128)(2,1)S(1)}, bf16[103,16,128]{2,1,0:T(8,128)(2,1)}, u32[]{:S(2)}) copy-start(bf16[103,16,128]{2,1,0:T(8,128)(2,1)} %get-tuple-element.144.refs_0_) | copy-start | bytes 1265668
  118.7 1.4 collective-permute-start.6
  141.3 6.0 %copy-start.1 = (f32[144,128]{1,0:T(8,128)S(1)}, f32[144,128]{1,0:T(8,128)}, u32[]{:S(2)}) copy-start(f32[144,128]{1,0:T(8,128)} %get-tuple-element.167) | copy-start | bytes 221188
  142.2 17.9 %all-to-all-start.5 = ((bf16[64,32,128]{2,1,0:T(8,128)(2,1)}), bf16[64,32,128]{2,1,0:T(8,128)(2,1)S(1)}, u32[]{:S(2)}, u32[]{:S(2)}) async-start(bf16[64,32,128]{2,1,0:T(8,128)(2,1)} %get-tuple-element.166), calls=%async_computation.5 | async-start | bytes 1048576 | tf_op jit(solution)/shard_map/all_to_all | solution.py:1002
  147.3 2.9 %collective-permute-start.7 = (f32[144,128]{1,0:T(8,128)S(1)}, f32[144,128]{1,0:T(8,128)S(1)}, u32[]{:S(2)}, u32[]{:S(2)}) collective-permute-start(f32[144,128]{1,0:T(8,128)S(1)} %copy-done.1), channel_id=1, source_target_pairs={{0,1},{1,0},{2,3},{3,2},{4,5},{5,4},{6,7},{7,6},{8,9},{9,8},{10,11... | collective-permute-start | bytes 221192 | tf_op jit(solution)/shard_map/ppermute | solution.py:886
  150.1 10.0 %collective-permute-start.8 = (f32[144,128]{1,0:T(8,128)S(1)}, f32[144,128]{1,0:T(8,128)S(1)}, u32[]{:S(2)}, u32[]{:S(2)}) collective-permute-start(f32[144,128]{1,0:T(8,128)S(1)} %broadcast_select_fusion), channel_id=1, source_target_pairs={{0,0},{1,31},{2,2},{3,29},{4,4},{5,27},{6,6},{7,25},{8,8},{9,23},{... | collective-permute-start | bytes 221192 | tf_op jit(solution)/shard_map/ppermute | solution.py:897
  160.1 2.7 %collective-permute-start.9 = (bf16[64,32,128]{2,1,0:T(8,128)(2,1)S(1)}, bf16[64,32,128]{2,1,0:T(8,128)(2,1)S(1)}, u32[]{:S(2)}, u32[]{:S(2)}) collective-permute-start(bf16[64,32,128]{2,1,0:T(8,128)(2,1)S(1)} %all-to-all-done.5.refs_0_), channel_id=1, source_target_pairs={{0,1},{1,0},{2,3},{3,2},{4,5},{5,4},{6,7},{7,6},{8,9},{9,8},{10,11... | collective-permute-start | bytes 1572872 | tf_op jit(solution)/shard_map/ppermute | solution.py:886
